TPU v7x, 256 devices: a whole 4x4x8 slice. The times are simulated.
256 devices in a mesh: slab: 64 (over y, x_lo, z), gy: 4 (over x_hi, core).
Axes of the slice: x: 4 (x_hi: 2, x_lo: 2; x = x_hi * 2 + x_lo), y: 4, z: 8, core: 2. Of those that a mesh axis runs over, the one named last changes fastest.
Arguments:
- field_in: bfloat16 [32, 192, 2, 32, 512], P(None, 'slab', None, None, 'gy'), may hold values from -6 to 6
- cotangent: bfloat16 [32, 192, 2, 32, 512], P(None, 'slab', None, None, 'gy'), may hold values from -6 to 6
- spectral_weight: bfloat16 [2, 3456, 32, 32], P(None, 'slab', None, 'gy'), may hold values from -0.75 to 0.75
- local_weight: bfloat16 [32, 32], replicated, may hold values from -1 to 1
Outputs:
- output: bfloat16 [32, 192, 2, 32, 512], P(None, 'slab', None, None, 'gy')
- grad_input: bfloat16 [32, 192, 2, 32, 512], P(None, 'slab', None, None, 'gy')
- grad_spectral: float32 [2, 3456, 32, 32], P(None, 'slab', None, 'gy')
- grad_local: float32 [32, 32], replicated
All inputs are finite; a program needn't handle non-finite values.
Results may differ from a plain program's by a relative error of at most 0.0053.
Values sent between devices are 32-bit elements; how exact they have to be, the bound alone decides.
A program may use at most 64 MiB of HBM per device.

v0:
```python
import math

import jax
import jax.numpy as jnp
from jax import lax
from jax.sharding import PartitionSpec as P

KX = 12
KY = 12
KZ = 12
NT = 2
NZ = 32


highest = lax.Precision.HIGHEST
root_half = 0.7071067811865476
inv_root_two_pi = 0.3989422804014327


def centred_frequencies(kept_count):
    values = jnp.arange(kept_count, dtype=jnp.int32)
    return jnp.where(values < kept_count // 2, values, values - kept_count)


def angle_table(row_count, length, kept_count, first_index):
    position = first_index + jnp.arange(row_count, dtype=jnp.int32)
    product = position[:, None] * centred_frequencies(kept_count)[None, :] % length
    phases = product.astype(jnp.float32) * (2.0 * math.pi / length)
    return (jnp.cos(phases), jnp.sin(phases))


def depth_tables(depth_count, level_count, kept_count):
    depth_pos = jnp.arange(depth_count, dtype=jnp.int32)
    level_pos = jnp.arange(level_count, dtype=jnp.int32)
    level_freq = jnp.arange(level_count, dtype=jnp.int32)
    depth_freq = centred_frequencies(kept_count)
    product = (
        level_pos[:, None, None, None] * level_freq[None, None, :, None] * depth_count
        + depth_pos[None, :, None, None] * depth_freq[None, None, None, :] * level_count
    ) % (depth_count * level_count)
    phases = product.astype(jnp.float32).reshape(
        level_count * depth_count, level_count * kept_count
    )
    phases = phases * (2.0 * math.pi / (depth_count * level_count))
    return (jnp.cos(phases), jnp.sin(phases))


def depth_forward(values, table):
    return jnp.einsum("crsk,sq->crkq", values, table, precision=highest)


def depth_inverse(values, table):
    return jnp.einsum("crkq,sq->crsk", values, table, precision=highest)


def rows_forward(values, table):
    return jnp.einsum("crkq,rp->pkqc", values, table, precision=highest)


def rows_inverse(values, table):
    return jnp.einsum("pkqc,rp->crkq", values, table, precision=highest)


def along_depth(field_data, y_table, depth_cos, depth_sin):
    channels, row_count = (field_data.shape[0], field_data.shape[1])
    kept_count = y_table.shape[1] // 2
    partial_value = jnp.dot(
        field_data.reshape(-1, field_data.shape[-1]), y_table, preferred_element_type=jnp.float32
    )
    partial_value = partial_value.reshape(channels, row_count, -1, 2, kept_count)
    cosine_part, sine_part = (partial_value[:, :, :, 0], partial_value[:, :, :, 1])
    real_part = depth_forward(cosine_part, depth_cos) + depth_forward(sine_part, depth_sin)
    imag_part = depth_forward(sine_part, depth_cos) - depth_forward(cosine_part, depth_sin)
    return (real_part, imag_part)


def along_rows(spectrum, row_cos, row_sin):
    real_part = rows_forward(spectrum[0], row_cos) + rows_forward(spectrum[1], row_sin)
    imag_part = rows_forward(spectrum[1], row_cos) - rows_forward(spectrum[0], row_sin)
    return (real_part.reshape(-1, real_part.shape[-1]), imag_part.reshape(-1, imag_part.shape[-1]))


def from_rows(spectrum, row_cos, row_sin):
    real_part = spectrum[0].reshape(KX, KY, NT * KZ, -1)
    imag_part = spectrum[1].reshape(KX, KY, NT * KZ, -1)
    first_out = rows_inverse(real_part, row_cos) - rows_inverse(imag_part, row_sin)
    second_out = rows_inverse(real_part, row_sin) + rows_inverse(imag_part, row_cos)
    return (first_out, second_out)


def from_depth(spectrum, y_table32, depth_cos, depth_sin):
    channels, row_count = (spectrum[0].shape[0], spectrum[0].shape[1])
    cosine_part = depth_inverse(spectrum[0], depth_cos) - depth_inverse(spectrum[1], depth_sin)
    sine_part = depth_inverse(spectrum[0], depth_sin) + depth_inverse(spectrum[1], depth_cos)
    stacked = jnp.concatenate([cosine_part, sine_part], axis=-1)
    field_data = jnp.dot(
        stacked.reshape(-1, stacked.shape[-1]),
        y_table32.T,
        precision=highest,
        preferred_element_type=jnp.float32,
    )
    return field_data.reshape(channels, row_count, NT, NZ, -1)


def mode_product(values, weight):
    return jnp.einsum("mi,mio->mo", values, weight, precision=highest)


def mode_adjoint(values, weight):
    return jnp.einsum("mo,mio->mi", values, weight, precision=highest)


def mode_outer(left, right):
    return jnp.einsum("mi,mo->mio", left, right, precision=highest)


def mix_modes(spectrum, weight):
    real_part = mode_product(spectrum[0], weight[0]) - mode_product(spectrum[1], weight[1])
    imag_part = mode_product(spectrum[0], weight[1]) + mode_product(spectrum[1], weight[0])
    return (real_part, imag_part)


def mix_back(spectrum, weight):
    real_part = mode_adjoint(spectrum[0], weight[0]) + mode_adjoint(spectrum[1], weight[1])
    imag_part = mode_adjoint(spectrum[1], weight[0]) - mode_adjoint(spectrum[0], weight[1])
    return (real_part, imag_part)


def weight_grad(mode_data, grad_modes):
    real_part = mode_outer(mode_data[0], grad_modes[0]) + mode_outer(mode_data[1], grad_modes[1])
    imag_part = mode_outer(mode_data[0], grad_modes[1]) - mode_outer(mode_data[1], grad_modes[0])
    return jnp.stack([real_part, imag_part])


def activate(values):
    return 0.5 * values * (1.0 + lax.erf(values * root_half))


def gelu_slope(values):
    return (
        0.5 * (1.0 + lax.erf(values * root_half))
        + values * jnp.exp(-0.5 * values * values) * inv_root_two_pi
    )


def per_device(field_in, cotangent, spectral_weight, local_weight):
    channels, row_count, level_count, depth_count, y_count = field_in.shape
    slab_count = lax.axis_size("slab")
    group_count = lax.axis_size("gy")
    quarter = channels // group_count
    first_lane = lax.axis_index("gy") * quarter
    slab_index = lax.axis_index("slab")
    total_x = row_count * slab_count
    total_y = y_count * group_count
    y_cos, y_sin = angle_table(y_count, total_y, KY, lax.axis_index("gy") * y_count)
    y_table32 = jnp.concatenate([y_cos, -y_sin], axis=1)
    y_table = y_table32.astype(jnp.bfloat16)
    depth_cos, depth_sin = depth_tables(depth_count, level_count, KZ)
    row_cos, row_sin = angle_table(row_count, total_x, KX, slab_index * row_count)
    forward_scale = 1.0 / math.sqrt(total_x * total_y * depth_count * level_count)
    inverse_scale = 1.0 / math.sqrt(KX * KY * KZ * NT)

    def to_modes(field_data, want_full):
        spectrum = along_depth(field_data, y_table, depth_cos, depth_sin)
        spectrum = along_rows(spectrum, row_cos, row_sin)
        spectrum = (
            lax.psum_scatter(spectrum[0], "slab", scatter_dimension=0, tiled=True),
            lax.psum_scatter(spectrum[1], "slab", scatter_dimension=0, tiled=True),
        )
        spectrum = lax.psum((spectrum[0], spectrum[1]), "gy")
        spectrum = (spectrum[0] * forward_scale, spectrum[1] * forward_scale)
        if want_full:
            return spectrum
        return (
            lax.dynamic_slice_in_dim(spectrum[0], first_lane, quarter, 1),
            lax.dynamic_slice_in_dim(spectrum[1], first_lane, quarter, 1),
        )

    def from_modes(spectrum):
        spectrum = (
            lax.all_gather(spectrum[0], "slab", axis=0, tiled=True),
            lax.all_gather(spectrum[1], "slab", axis=0, tiled=True),
        )
        spectrum = from_rows(spectrum, row_cos, row_sin)
        spectrum = (
            lax.all_gather(spectrum[0], "gy", axis=0, tiled=True),
            lax.all_gather(spectrum[1], "gy", axis=0, tiled=True),
        )
        return from_depth(spectrum, y_table32, depth_cos, depth_sin) * inverse_scale

    weight = spectral_weight.astype(jnp.float32)
    mode_data = to_modes(field_in, True)
    mixed_modes = mix_modes(mode_data, weight)
    spectral = from_modes(mixed_modes)
    flat_in = field_in.reshape(channels, -1)
    local_part = jnp.dot(local_weight.T, flat_in, preferred_element_type=jnp.float32).reshape(
        field_in.shape
    )
    pre_act = spectral + local_part
    output = activate(pre_act).astype(jnp.bfloat16)
    grad_pre = (cotangent.astype(jnp.float32) * gelu_slope(pre_act)).astype(jnp.bfloat16)
    grad_modes = to_modes(grad_pre, False)
    grad_spectral = weight_grad(mode_data, grad_modes)
    back_modes = mix_back(grad_modes, weight)
    back_modes = (
        lax.psum_scatter(back_modes[0], "gy", scatter_dimension=1, tiled=True),
        lax.psum_scatter(back_modes[1], "gy", scatter_dimension=1, tiled=True),
    )
    flat_grad = grad_pre.reshape(channels, -1)
    local_terms = lax.dot_general(
        flat_in, flat_grad, (((1,), (1,)), ((), ())), preferred_element_type=jnp.float32
    )
    grad_local = lax.psum(local_terms, ("slab", "gy")) * forward_scale
    local_back = jnp.dot(local_weight, flat_grad, preferred_element_type=jnp.float32).reshape(
        field_in.shape
    )
    grad_input = (from_modes(back_modes) + local_back).astype(jnp.bfloat16)
    return (output, grad_input, grad_spectral, grad_local)


def solution(mesh):
    placed = (
        P(None, "slab", None, None, "gy"),
        P(None, "slab", None, None, "gy"),
        P(None, "slab", None, "gy"),
        P(),
    )
    return jax.shard_map(
        per_device,
        mesh=mesh,
        in_specs=placed,
        out_specs=(
            P(None, "slab", None, None, "gy"),
            P(None, "slab", None, None, "gy"),
            P(None, "slab", None, "gy"),
            P(),
        ),
        check_vma=False,
    )
```

profile of v0, /device:TPU:1, one launch (start us, length us, event | category | flops | bytes accessed | tf_op | source)
XLA Modules:
  0.0 1441.1 jit_solution(13167168765521243251)
XLA Ops:
  14.8 2.4 fusion.56
  17.2 2.7 fusion.60
  19.9 2.6 subtract_bitcast_fusion.1
  23.1 2.5 add_bitcast_fusion.1
  26.2 160.4 %fusion.226 = (f32[64,32]{1,0:T(8,128)}, f32[64,32]{1,0:T(8,128)}) fusion(f32[3456,32]{1,0:T(8,128)S(1)} %bitcast.242, f32[3456,32]{1,0:T(8,128)S(1)} %bitcast.244), kind=kCustom, calls=%all-reduce-scatter.5 | all-reduce-scatter fusion | flops 262145 | bytes 902144
  193.8 2.4 copy.291
  196.7 2.7 fusion.23
  202.0 3.2 collective-permute-start.12
  205.2 5.2 collective-permute-start.11
  210.5 3.1 collective-permute-start.10
  213.7 15.3 %collective-permute-start.8 = (f32[64,32]{1,0:T(8,128)S(1)}, f32[64,32]{1,0:T(8,128)S(1)}, u32[]{:S(2)}, u32[]{:S(2)}) collective-permute-start(f32[64,32]{1,0:T(8,128)S(1)} %copy-done.15), channel_id=1, source_target_pairs={{0,36},{4,40},{8,44},{12,48},{16,52},{20,56},{24,60},{28,64},{32,6... | collective-permute-start | bytes 24584
  230.9 3.4 collective-permute-start.6
  234.4 2.5 collective-permute-start.5
  236.9 3.1 collective-permute-start.9
  244.9 2.9 collective-permute-start.4
  247.8 4.3 collective-permute-start.3
  252.2 4.0 collective-permute-start.2
  256.2 3.2 collective-permute-start.1
  259.3 2.6 collective-permute-start
  264.7 48.4 %all-reduce.12 = (f32[54,32]{1,0:T(8,128)S(1)}, f32[54,32]{1,0:T(8,128)S(1)}) all-reduce(f32[54,32]{1,0:T(8,128)S(1)} %constant_dynamic-slice_fusion.2, f32[54,32]{1,0:T(8,128)S(1)} %constant_dynamic-slice_fusion.3), channel_id=1, replica_groups=mesh['slab'=64,'gy'=4] {'gy'}, use_global_device_ids=true, to_apply=%region_3.4 | all-reduce | flops 3456 | bytes 27648 | tf_op jit(solution)/shard_map/psum | solution.py:170
  313.4 134.8 %all-gather = f32[64,54,8]{1,2,0:T(8,128)S(1)} all-gather(f32[1,54,8]{1,2,0:T(8,128)S(1)} %subtract_bitcast_fusion.3), channel_id=1, replica_groups=mesh['slab'=64,'gy'=4] {'slab'}, dimensions={0}, use_global_device_ids=true | all-gather | bytes 112320 | tf_op jit(solution)/shard_map/all_gather | solution.py:181
  450.2 123.6 %all-gather.1 = f32[64,54,8]{1,2,0:T(8,128)S(1)} all-gather(f32[1,54,8]{1,2,0:T(8,128)S(1)} %add_bitcast_fusion.3), channel_id=1, replica_groups=mesh['slab'=64,'gy'=4] {'slab'}, dimensions={0}, use_global_device_ids=true | all-gather | bytes 112320 | tf_op jit(solution)/shard_map/all_gather | solution.py:182
  575.0 66.1 %all_gather.26 = f32[32,3,12,24]{3,1,0,2:T(4,128)S(1)} all-gather(f32[8,3,12,24]{3,1,0,2:T(4,128)S(1)} %fusion.29), channel_id=1, replica_groups=mesh['slab'=64,'gy'=4] {'gy'}, dimensions={0}, use_global_device_ids=true | all-gather | bytes 138240 | tf_op jit(solution)/shard_map/all_gather | solution.py:186
  643.2 10.2 all_gather.27
  656.3 10.3 fusion.9
  671.4 2.4 fusion.74
  673.8 2.4 convolution_subtract_fusion.2
  676.3 2.4 convolution_add_fusion.2
  678.7 2.4 fusion.54
  681.1 2.6 fusion.50
  683.7 2.6 add_bitcast_fusion
  686.9 2.5 subtract_bitcast_fusion
  690.0 153.9 %fusion.225 = (f32[64,32]{1,0:T(8,128)}, f32[64,32]{1,0:T(8,128)}) fusion(f32[3456,32]{1,0:T(8,128)S(1)} %bitcast.243, f32[3456,32]{1,0:T(8,128)S(1)} %bitcast.245), kind=kCustom, calls=%all-reduce-scatter.4 | all-reduce-scatter fusion | flops 262145 | bytes 902144
  851.2 3.6 fusion.33
  854.8 106.8 %psum.39 = f32[32,32]{0,1:T(8,128)S(1)} all-reduce(f32[32,32]{0,1:T(8,128)S(1)} %fusion.33), channel_id=1, replica_groups=mesh['slab'=64,'gy'=4] {'slab','gy'}, use_global_device_ids=true, to_apply=%region_10.11 | all-reduce | flops 1024 | bytes 8192 | tf_op jit(solution)/shard_map/psum | solution.py:213
  961.7 2.6 collective-permute-start.24
  964.3 4.0 collective-permute-start.23
  968.3 3.0 collective-permute-start.22
  971.4 3.1 collective-permute-start.21
  974.5 3.1 collective-permute-start.20
  978.3 4.7 collective-permute-start.38
  983.1 4.2 collective-permute-start.37
  987.3 2.7 collective-permute-start.36
  990.0 4.3 collective-permute-start.35
  994.3 2.9 collective-permute-start.39
  997.3 2.7 convolution_bitcast_fusion.1
  1000.7 2.5 copy.202
  1003.1 15.5 %concatenate.14 = f32[694,32]{1,0:T(8,128)} concatenate(f32[54,32]{1,0:T(8,128)} %copy-done.39, f32[64,32]{1,0:T(8,128)S(1)} %collective-permute-done.28, f32[64,32]{1,0:T(8,128)S(1)} %collective-permute-done.27, f32[64,32]{1,0:T(8,128)S(1)} %collective-permute-done.26, f32[64,32]{1,0:T(8,128)} %copy-done.32, f32[64,32]{1,0:T(8,128)} %copy-done.33, f32[64,32]{1,0:T(8,128)} %copy-done.34, ...), dimensions={0} | concatenate | bytes 177664
  1018.6 4.9 collective-permute-start.34
  1023.6 4.9 collective-permute-start.33
  1028.5 2.5 collective-permute-start.32
  1031.0 4.2 collective-permute-start.31
  1035.2 2.9 collective-permute-start.30
  1039.6 15.2 %concatenate.15 = f32[694,32]{1,0:T(8,128)} concatenate(f32[54,32]{1,0:T(8,128)} %collective-permute-done.39, f32[64,32]{1,0:T(8,128)S(1)} %collective-permute-done.38, f32[64,32]{1,0:T(8,128)S(1)} %collective-permute-done.37, f32[64,32]{1,0:T(8,128)} %collective-permute-done.36, f32[64,32]{1,0:T(8,128)} %collective-permute-done.35, f32[64,32]{1,0:T(8,128)S(1)} %collective-permute-done.34, ...), dimensions={0} | concatenate | bytes 177664
  1055.6 17.8 %all-reduce.11 = (f32[54,32]{1,0:T(8,128)S(1)}, f32[54,32]{1,0:T(8,128)S(1)}) all-reduce(f32[54,32]{1,0:T(8,128)S(1)} %constant_dynamic-slice_fusion.1, f32[54,32]{1,0:T(8,128)S(1)} %constant_dynamic-slice_fusion), channel_id=1, replica_groups=mesh['slab'=64,'gy'=4] {'gy'}, use_global_device_ids=true, to_apply=%region_5.6 | all-reduce | flops 3456 | bytes 27648 | tf_op jit(solution)/shard_map/psum | solution.py:170
  1074.7 13.3 all-reduce.10
  1088.0 125.6 %all-gather.2 = f32[64,54,8]{1,2,0:T(8,128)S(1)} all-gather(f32[1,54,8]{1,2,0:T(8,128)S(1)} %dynamic-slice_bitcast_fusion.1), channel_id=1, replica_groups=mesh['slab'=64,'gy'=4] {'slab'}, dimensions={0}, use_global_device_ids=true | all-gather | bytes 112320 | tf_op jit(solution)/shard_map/all_gather | solution.py:181
  1214.9 2.6 fusion.40
  1217.5 2.6 fusion.42
  1220.0 123.8 %all-gather.3 = f32[64,54,8]{1,2,0:T(8,128)S(1)} all-gather(f32[1,54,8]{1,2,0:T(8,128)S(1)} %dynamic-slice_bitcast_fusion), channel_id=1, replica_groups=mesh['slab'=64,'gy'=4] {'slab'}, dimensions={0}, use_global_device_ids=true | all-gather | bytes 112320 | tf_op jit(solution)/shard_map/all_gather | solution.py:182
  1347.1 65.4 %all_gather.30 = f32[32,3,12,24]{3,1,0,2:T(4,128)S(1)} all-gather(f32[8,3,12,24]{3,1,0,2:T(4,128)S(1)} %fusion.31), channel_id=1, replica_groups=mesh['slab'=64,'gy'=4] {'gy'}, dimensions={0}, use_global_device_ids=true | all-gather | bytes 138240 | tf_op jit(solution)/shard_map/all_gather | solution.py:186
  1414.7 10.2 all_gather.31
  1427.4 3.9 dot_general.232
  1432.0 8.6 add_convert_fusion
  (225 shorter events, 69.7 us)
Async XLA Ops:
  0.6 196.0 %copy-start = (bf16[32,32]{1,0:T(8,128)(2,1)S(1)}, bf16[32,32]{1,0:T(8,128)(2,1)}, u32[]{:S(2)}) copy-start(bf16[32,32]{1,0:T(8,128)(2,1)} %param.7) | copy-start | bytes 6148
  1.5 10.9 copy-start.11
  186.6 14.1 collective-permute-start.18
  187.9 14.1 collective-permute-start.17
  189.2 16.1 %collective-permute-start.16 = (f32[64,32]{1,0:T(8,128)}, f32[64,32]{1,0:T(8,128)S(1)}, u32[]{:S(2)}, u32[]{:S(2)}) collective-permute-start(f32[64,32]{1,0:T(8,128)} %get-tuple-element.40), channel_id=1, source_target_pairs={{0,28},{4,32},{8,36},{12,40},{16,44},{20,48},{24,52},{28,56},{32,6... | collective-permute-start | bytes 24584
  190.5 20.0 %collective-permute-start.15 = (f32[64,32]{1,0:T(8,128)}, f32[64,32]{1,0:T(8,128)S(1)}, u32[]{:S(2)}, u32[]{:S(2)}) collective-permute-start(f32[64,32]{1,0:T(8,128)} %get-tuple-element.40), channel_id=1, source_target_pairs={{0,24},{4,28},{8,32},{12,36},{16,40},{20,44},{24,48},{28,52},{32,5... | collective-permute-start | bytes 24584
  192.5 6.9 collective-permute-start.19
  196.6 17.0 %copy-start.30 = (s32[32,12]{0,1:T(8,128)S(1)}, s32[32,12]{0,1:T(8,128)}, u32[]{:S(2)}) copy-start(s32[32,12]{0,1:T(8,128)} %copy-done.29) | copy-start | bytes 4612
  196.6 17.0 %copy-start.41 = (s32[2,2]{0,1:T(2,128)S(1)}, s32[2,2]{0,1:T(2,128)}, u32[]{:S(2)}) copy-start(s32[2,2]{0,1:T(2,128)} %copy-done.40) | copy-start | bytes 52
  196.6 17.0 %copy-start.15 = (f32[64,32]{1,0:T(8,128)S(1)}, f32[64,32]{1,0:T(8,128)}, u32[]{:S(2)}) copy-start(f32[64,32]{1,0:T(8,128)} %get-tuple-element.41) | copy-start | bytes 24580
  196.7 43.4 %copy-start.24 = (f32[128,12]{0,1:T(8,128)S(1)}, f32[128,12]{0,1:T(8,128)}, u32[]{:S(2)}) copy-start(f32[128,12]{0,1:T(8,128)} %copy-done.23) | copy-start | bytes 18436
  196.7 43.4 %copy-start.27 = (f32[128,12]{0,1:T(8,128)S(1)}, f32[128,12]{0,1:T(8,128)}, u32[]{:S(2)}) copy-start(f32[128,12]{0,1:T(8,128)} %copy-done.26) | copy-start | bytes 18436
  196.7 43.4 %copy-start.42 = (u32[256]{0:T(256)S(1)}, u32[256]{0:T(256)}, u32[]{:S(2)}) copy-start(u32[256]{0:T(256)} %constant.102) | copy-start | bytes 3076
  196.7 44.7 %copy-start.43 = (u32[256]{0:T(256)S(1)}, u32[256]{0:T(256)}, u32[]{:S(2)}) copy-start(u32[256]{0:T(256)} %constant.118) | copy-start | bytes 3076
  196.7 116.6 %copy-start.7 = (bf16[2,54,32,8]{1,3,2,0:T(8,128)(2,1)S(1)}, bf16[2,54,32,8]{1,3,2,0:T(8,128)(2,1)}, u32[]{:S(2)}) copy-start(bf16[2,54,32,8]{1,3,2,0:T(8,128)(2,1)} %param.6) | copy-start | bytes 165892
  199.4 14.3 collective-permute-start.14
  200.7 28.3 %collective-permute-start.13 = (f32[64,32]{1,0:T(8,128)S(1)}, f32[64,32]{1,0:T(8,128)S(1)}, u32[]{:S(2)}, u32[]{:S(2)}) collective-permute-start(f32[64,32]{1,0:T(8,128)S(1)} %copy-done.17), channel_id=1, source_target_pairs={{0,16},{4,20},{8,24},{12,28},{16,32},{20,36},{24,40},{28,44},{32,4... | collective-permute-start | bytes 24584
  202.0 28.9 %collective-permute-start.12 = (f32[64,32]{1,0:T(8,128)S(1)}, f32[64,32]{1,0:T(8,128)S(1)}, u32[]{:S(2)}, u32[]{:S(2)}) collective-permute-start(f32[64,32]{1,0:T(8,128)S(1)} %copy-done.17), channel_id=1, source_target_pairs={{0,12},{4,16},{8,20},{12,24},{16,28},{20,32},{24,36},{28,40},{32,4... | collective-permute-start | bytes 24584
  205.2 29.1 %collective-permute-start.11 = (f32[64,32]{1,0:T(8,128)S(1)}, f32[64,32]{1,0:T(8,128)S(1)}, u32[]{:S(2)}, u32[]{:S(2)}) collective-permute-start(f32[64,32]{1,0:T(8,128)S(1)} %copy-done.17), channel_id=1, source_target_pairs={{0,8},{4,12},{8,16},{12,20},{16,24},{20,28},{24,32},{28,36},{32,40... | collective-permute-start | bytes 24584
  210.5 26.4 %collective-permute-start.10 = (f32[64,32]{1,0:T(8,128)S(1)}, f32[64,32]{1,0:T(8,128)S(1)}, u32[]{:S(2)}, u32[]{:S(2)}) collective-permute-start(f32[64,32]{1,0:T(8,128)S(1)} %copy-done.17), channel_id=1, source_target_pairs={{0,4},{4,8},{8,12},{12,16},{16,20},{20,24},{24,28},{28,32},{32,36}... | collective-permute-start | bytes 24584
  213.7 34.1 %collective-permute-start.8 = (f32[64,32]{1,0:T(8,128)S(1)}, f32[64,32]{1,0:T(8,128)S(1)}, u32[]{:S(2)}, u32[]{:S(2)}) collective-permute-start(f32[64,32]{1,0:T(8,128)S(1)} %copy-done.15), channel_id=1, source_target_pairs={{0,36},{4,40},{8,44},{12,48},{16,52},{20,56},{24,60},{28,64},{32,6... | collective-permute-start | bytes 24584
  229.0 23.2 %collective-permute-start.7 = (f32[64,32]{1,0:T(8,128)S(1)}, f32[64,32]{1,0:T(8,128)S(1)}, u32[]{:S(2)}, u32[]{:S(2)}) collective-permute-start(f32[64,32]{1,0:T(8,128)S(1)} %copy-done.15), channel_id=1, source_target_pairs={{0,32},{4,36},{8,40},{12,44},{16,48},{20,52},{24,56},{28,60},{32,6... | collective-permute-start | bytes 24584
  230.9 25.2 %collective-permute-start.6 = (f32[64,32]{1,0:T(8,128)S(1)}, f32[64,32]{1,0:T(8,128)S(1)}, u32[]{:S(2)}, u32[]{:S(2)}) collective-permute-start(f32[64,32]{1,0:T(8,128)S(1)} %copy-done.15), channel_id=1, source_target_pairs={{0,28},{4,32},{8,36},{12,40},{16,44},{20,48},{24,52},{28,56},{32,6... | collective-permute-start | bytes 24584
  234.4 25.0 %collective-permute-start.5 = (f32[64,32]{1,0:T(8,128)S(1)}, f32[64,32]{1,0:T(8,128)S(1)}, u32[]{:S(2)}, u32[]{:S(2)}) collective-permute-start(f32[64,32]{1,0:T(8,128)S(1)} %copy-done.15), channel_id=1, source_target_pairs={{0,24},{4,28},{8,32},{12,36},{16,40},{20,44},{24,48},{28,52},{32,5... | collective-permute-start | bytes 24584
  236.9 8.0 collective-permute-start.9
  241.4 412.8 %copy-start.4 = (s32[64,24]{0,1:T(8,128)}, s32[64,24]{0,1:T(8,128)S(1)}, u32[]{:S(2)}) copy-start(s32[64,24]{0,1:T(8,128)S(1)} %add.368) | copy-start | bytes 18436
  244.9 17.1 %collective-permute-start.4 = (f32[64,32]{1,0:T(8,128)S(1)}, f32[64,32]{1,0:T(8,128)S(1)}, u32[]{:S(2)}, u32[]{:S(2)}) collective-permute-start(f32[64,32]{1,0:T(8,128)S(1)} %copy-done.15), channel_id=1, source_target_pairs={{0,20},{4,24},{8,28},{12,32},{16,36},{20,40},{24,44},{28,48},{32,5... | collective-permute-start | bytes 24584
  247.8 14.2 collective-permute-start.3
  252.2 9.9 collective-permute-start.2
  256.2 5.9 collective-permute-start.1
  259.3 3.7 collective-permute-start
  313.2 135.0 %copy-start.19 = (f32[54,32]{0,1:T(8,128)}, f32[54,32]{0,1:T(8,128)S(1)}, u32[]{:S(2)}) copy-start(f32[54,32]{0,1:T(8,128)S(1)} %copy.192) | copy-start | bytes 20740
  313.3 134.9 %copy-start.21 = (f32[54,32]{0,1:T(8,128)}, f32[54,32]{0,1:T(8,128)S(1)}, u32[]{:S(2)}) copy-start(f32[54,32]{0,1:T(8,128)S(1)} %copy.191) | copy-start | bytes 20740
  843.8 117.8 %copy-start.18 = (f32[64,32]{1,0:T(8,128)S(1)}, f32[64,32]{1,0:T(8,128)}, u32[]{:S(2)}) copy-start(f32[64,32]{1,0:T(8,128)} %get-tuple-element.36) | copy-start | bytes 24580
  843.8 133.9 %copy-start.16 = (f32[64,32]{1,0:T(8,128)S(1)}, f32[64,32]{1,0:T(8,128)}, u32[]{:S(2)}) copy-start(f32[64,32]{1,0:T(8,128)} %get-tuple-element.37) | copy-start | bytes 24580
  843.8 153.5 %copy-start.3 = (bf16[32,3,2,32,128]{4,3,2,1,0:T(8,128)(2,1)S(1)}, bf16[32,3,2,32,128]{4,3,2,1,0:T(8,128)(2,1)}, u32[]{:S(2)}) copy-start(bf16[32,3,2,32,128]{4,3,2,1,0:T(8,128)(2,1)} %copy-done.2) | copy-start | bytes 4718596
  844.7 119.6 %collective-permute-start.28 = (f32[64,32]{1,0:T(8,128)}, f32[64,32]{1,0:T(8,128)S(1)}, u32[]{:S(2)}, u32[]{:S(2)}) collective-permute-start(f32[64,32]{1,0:T(8,128)} %get-tuple-element.36), channel_id=1, source_target_pairs={{0,36},{4,40},{8,44},{12,48},{16,52},{20,56},{24,60},{28,64},{32,6... | collective-permute-start | bytes 24584
  846.0 122.4 %collective-permute-start.27 = (f32[64,32]{1,0:T(8,128)}, f32[64,32]{1,0:T(8,128)S(1)}, u32[]{:S(2)}, u32[]{:S(2)}) collective-permute-start(f32[64,32]{1,0:T(8,128)} %get-tuple-element.36), channel_id=1, source_target_pairs={{0,32},{4,36},{8,40},{12,44},{16,48},{20,52},{24,56},{28,60},{32,6... | collective-permute-start | bytes 24584
  847.3 124.1 %collective-permute-start.26 = (f32[64,32]{1,0:T(8,128)}, f32[64,32]{1,0:T(8,128)S(1)}, u32[]{:S(2)}, u32[]{:S(2)}) collective-permute-start(f32[64,32]{1,0:T(8,128)} %get-tuple-element.36), channel_id=1, source_target_pairs={{0,28},{4,32},{8,36},{12,40},{16,44},{20,48},{24,52},{28,56},{32,6... | collective-permute-start | bytes 24584
  848.6 125.9 %collective-permute-start.25 = (f32[64,32]{1,0:T(8,128)}, f32[64,32]{1,0:T(8,128)S(1)}, u32[]{:S(2)}, u32[]{:S(2)}) collective-permute-start(f32[64,32]{1,0:T(8,128)} %get-tuple-element.36), channel_id=1, source_target_pairs={{0,24},{4,28},{8,32},{12,36},{16,40},{20,44},{24,48},{28,52},{32,5... | collective-permute-start | bytes 24584
  849.9 111.8 %collective-permute-start.29 = (f32[54,32]{1,0:T(8,128)S(1)}, f32[54,32]{1,0:T(8,128)S(1)}, u32[]{:S(2)}, u32[]{:S(2)}) collective-permute-start(f32[54,32]{1,0:T(8,128)S(1)} %slice.36), channel_id=1, source_target_pairs={{0,40},{4,44},{8,48},{12,52},{16,56},{20,60},{24,64},{28,68},{32,7... | collective-permute-start | bytes 20744
  961.7 16.7 %collective-permute-start.24 = (f32[64,32]{1,0:T(8,128)S(1)}, f32[64,32]{1,0:T(8,128)S(1)}, u32[]{:S(2)}, u32[]{:S(2)}) collective-permute-start(f32[64,32]{1,0:T(8,128)S(1)} %copy-done.18), channel_id=1, source_target_pairs={{0,20},{4,24},{8,28},{12,32},{16,36},{20,40},{24,44},{28,48},{32,5... | collective-permute-start | bytes 24584
  964.3 18.7 %collective-permute-start.23 = (f32[64,32]{1,0:T(8,128)S(1)}, f32[64,32]{1,0:T(8,128)S(1)}, u32[]{:S(2)}, u32[]{:S(2)}) collective-permute-start(f32[64,32]{1,0:T(8,128)S(1)} %copy-done.18), channel_id=1, source_target_pairs={{0,16},{4,20},{8,24},{12,28},{16,32},{20,36},{24,40},{28,44},{32,4... | collective-permute-start | bytes 24584
  968.3 19.0 %collective-permute-start.22 = (f32[64,32]{1,0:T(8,128)S(1)}, f32[64,32]{1,0:T(8,128)S(1)}, u32[]{:S(2)}, u32[]{:S(2)}) collective-permute-start(f32[64,32]{1,0:T(8,128)S(1)} %copy-done.18), channel_id=1, source_target_pairs={{0,12},{4,16},{8,20},{12,24},{16,28},{20,32},{24,36},{28,40},{32,4... | collective-permute-start | bytes 24584
  971.4 18.6 %collective-permute-start.21 = (f32[64,32]{1,0:T(8,128)S(1)}, f32[64,32]{1,0:T(8,128)S(1)}, u32[]{:S(2)}, u32[]{:S(2)}) collective-permute-start(f32[64,32]{1,0:T(8,128)S(1)} %copy-done.18), channel_id=1, source_target_pairs={{0,8},{4,12},{8,16},{12,20},{16,24},{20,28},{24,32},{28,36},{32,40... | collective-permute-start | bytes 24584
  974.5 19.8 %collective-permute-start.20 = (f32[64,32]{1,0:T(8,128)S(1)}, f32[64,32]{1,0:T(8,128)S(1)}, u32[]{:S(2)}, u32[]{:S(2)}) collective-permute-start(f32[64,32]{1,0:T(8,128)S(1)} %copy-done.18), channel_id=1, source_target_pairs={{0,4},{4,8},{8,12},{12,16},{16,20},{20,24},{24,28},{28,32},{32,36}... | collective-permute-start | bytes 24584
  978.3 45.2 %collective-permute-start.38 = (f32[64,32]{1,0:T(8,128)S(1)}, f32[64,32]{1,0:T(8,128)S(1)}, u32[]{:S(2)}, u32[]{:S(2)}) collective-permute-start(f32[64,32]{1,0:T(8,128)S(1)} %copy-done.16), channel_id=1, source_target_pairs={{0,36},{4,40},{8,44},{12,48},{16,52},{20,56},{24,60},{28,64},{32,6... | collective-permute-start | bytes 24584
  983.1 16.9 %copy-start.34 = (f32[64,32]{1,0:T(8,128)}, f32[64,32]{1,0:T(8,128)S(1)}, u32[]{:S(2)}) copy-start(f32[64,32]{1,0:T(8,128)S(1)} %collective-permute-done.23) | copy-start | bytes 24580
  983.1 45.4 %collective-permute-start.37 = (f32[64,32]{1,0:T(8,128)S(1)}, f32[64,32]{1,0:T(8,128)S(1)}, u32[]{:S(2)}, u32[]{:S(2)}) collective-permute-start(f32[64,32]{1,0:T(8,128)S(1)} %copy-done.16), channel_id=1, source_target_pairs={{0,32},{4,36},{8,40},{12,44},{16,48},{20,52},{24,56},{28,60},{32,6... | collective-permute-start | bytes 24584
  987.3 12.6 copy-start.35
  987.3 43.7 %collective-permute-start.36 = (f32[64,32]{1,0:T(8,128)S(1)}, f32[64,32]{1,0:T(8,128)}, u32[]{:S(2)}, u32[]{:S(2)}) collective-permute-start(f32[64,32]{1,0:T(8,128)S(1)} %copy-done.16), channel_id=1, source_target_pairs={{0,28},{4,32},{8,36},{12,40},{16,44},{20,48},{24,52},{28,56},{32,6... | collective-permute-start | bytes 24584
  990.0 45.2 %collective-permute-start.35 = (f32[64,32]{1,0:T(8,128)S(1)}, f32[64,32]{1,0:T(8,128)}, u32[]{:S(2)}, u32[]{:S(2)}) collective-permute-start(f32[64,32]{1,0:T(8,128)S(1)} %copy-done.16), channel_id=1, source_target_pairs={{0,24},{4,28},{8,32},{12,36},{16,40},{20,44},{24,48},{28,52},{32,5... | collective-permute-start | bytes 24584
  994.3 24.3 %collective-permute-start.39 = (f32[54,32]{1,0:T(8,128)}, f32[54,32]{1,0:T(8,128)}, u32[]{:S(2)}, u32[]{:S(2)}) collective-permute-start(f32[54,32]{1,0:T(8,128)} %slice.37), channel_id=1, source_target_pairs={{0,40},{4,44},{8,48},{12,52},{16,56},{20,60},{24,64},{28,68},{32,7... | collective-permute-start | bytes 20744
  1000.6 73.0 %copy-start.8 = (bf16[2,54,32,8]{1,3,2,0:T(8,128)(2,1)S(1)}, bf16[2,54,32,8]{1,3,2,0:T(8,128)(2,1)}, u32[]{:S(2)}) copy-start(bf16[2,54,32,8]{1,3,2,0:T(8,128)(2,1)} %param.6) | copy-start | bytes 165892
  1000.6 73.2 %copy-start.20 = (f32[54,32]{0,1:T(8,128)S(1)}, f32[54,32]{0,1:T(8,128)}, u32[]{:S(2)}) copy-start(f32[54,32]{0,1:T(8,128)} %copy-done.19) | copy-start | bytes 20740
  1000.6 73.2 %copy-start.22 = (f32[54,32]{0,1:T(8,128)S(1)}, f32[54,32]{0,1:T(8,128)}, u32[]{:S(2)}) copy-start(f32[54,32]{0,1:T(8,128)} %copy-done.21) | copy-start | bytes 20740
  1018.6 20.3 %collective-permute-start.34 = (f32[64,32]{1,0:T(8,128)S(1)}, f32[64,32]{1,0:T(8,128)S(1)}, u32[]{:S(2)}, u32[]{:S(2)}) collective-permute-start(f32[64,32]{1,0:T(8,128)S(1)} %copy-done.16), channel_id=1, source_target_pairs={{0,20},{4,24},{8,28},{12,32},{16,36},{20,40},{24,44},{28,48},{32,5... | collective-permute-start | bytes 24584
  1023.6 15.4 %collective-permute-start.33 = (f32[64,32]{1,0:T(8,128)S(1)}, f32[64,32]{1,0:T(8,128)S(1)}, u32[]{:S(2)}, u32[]{:S(2)}) collective-permute-start(f32[64,32]{1,0:T(8,128)S(1)} %copy-done.16), channel_id=1, source_target_pairs={{0,16},{4,20},{8,24},{12,28},{16,32},{20,36},{24,40},{28,44},{32,4... | collective-permute-start | bytes 24584
  1028.5 10.4 collective-permute-start.32
  1031.0 7.9 collective-permute-start.31
  1035.2 4.4 collective-permute-start.30
  1217.5 195.1 %copy-start.5 = (s32[64,24]{0,1:T(8,128)S(1)}, s32[64,24]{0,1:T(8,128)}, u32[]{:S(2)}) copy-start(s32[64,24]{0,1:T(8,128)} %copy-done.4) | copy-start | bytes 18436
  1345.1 68.7 %copy-start.1 = (f32[12,12,24,8]{2,1,0,3:T(8,128)S(1)}, f32[12,12,24,8]{2,1,0,3:T(8,128)}, u32[]{:S(2)}) copy-start(f32[12,12,24,8]{2,1,0,3:T(8,128)} %reshape.188) | copy-start | bytes 331780
  1345.1 68.8 %copy-start.6 = (f32[3,12,24,8]{2,0,3,1:T(4,128)S(1)}, f32[3,12,24,8]{2,0,3,1:T(4,128)}, u32[]{:S(2)}) copy-start(f32[3,12,24,8]{2,0,3,1:T(4,128)} %fusion.40) | copy-start | bytes 82948
  (20 other events, 88.8 us)
where the time goes:
time: 1450 us; the launch traced here: 1440 us
  blocking collectives  1160 us (80%)
  starting transfers between devices  124 us (9%)
  matrix products  87.6 us (6%)
  local copies, waits for them, and re-layouts  59.7 us (4%)
    unnamed x3, blocking collectives  328 us
    all_gather x2, blocking collectives, from_modes(): lax.all_gather(spectrum[0], 'slab', axis=0, tiled=True)  260 us
    all_gather x2, blocking collectives, from_modes(): lax.all_gather(spectrum[1], 'slab', axis=0, tiled=True)  247 us
    all_gather x2, blocking collectives, from_modes(): lax.all_gather(spectrum[0], 'gy', axis=0, tiled=True)  131 us
    unnamed x40, starting transfers between devices  124 us
    psum x1, blocking collectives, per_device(): grad_local = lax.psum(local_terms, ('slab', 'gy')) * forward_scale  107 us
    psum x2, blocking collectives, to_modes(): spectrum = lax.psum((spectrum[0], spectrum[1]), 'gy')  66.2 us
    unnamed x112, local copies, waits for them, and re-layouts  46.6 us
  transfers between devices with their start and end apart: 40, of which 1 were waited for; matrix products, arithmetic and copies ran while one was open for 3% of the time, Pallas kernels for 0%

commit v1 on v0

v1 whole, which is shorter than its diff:
```python
import functools
import math

import jax
import jax.numpy as jnp
import numpy as np
from jax import lax
from jax.experimental import pallas as pl
from jax.experimental.pallas import tpu as pltpu
from jax.sharding import PartitionSpec as P

C = 32
KX = 12
KY = 12
KZ = 12
NT = 2
NZ = 32
NX = 192
NY = 512
CX = 3
N_GY = 4
N_Y = 4
N_R = 16
Q = C // N_GY
K = NT * KZ
TZ = NT * NZ
Y = NY // N_GY
BLOCK = 54
UNITS = 9
ROWS = 72
LANES = K * Q

FORWARD_SCALE = 1.0 / math.sqrt(NX * NY * NZ * NT)
INVERSE_SCALE = 1.0 / math.sqrt(KX * KY * KZ * NT)
ROOT_HALF = 0.7071067811865476
INV_ROOT_TWO_PI = 0.3989422804014327
HIGHEST = lax.Precision.HIGHEST
F32 = jnp.float32
BF16 = jnp.bfloat16
MESH = pl.DeviceIdType.MESH


def frequencies(kept):
    values = np.arange(kept)
    return np.where(values < kept // 2, values, values - kept)


def depth_table():
    t, z = np.divmod(np.arange(TZ), NZ)
    kt, kz = np.divmod(np.arange(K), KZ)
    product = (t[None] * kt[:, None] * NZ + z[None] * frequencies(KZ)[kz][:, None] * NT) % TZ
    angle = product * (2.0 * np.pi / TZ)
    parts = np.stack([np.cos(angle), -np.sin(angle)])
    full = np.einsum("pks,cd->pkcds", parts, np.eye(Q))
    return full.reshape(2 * K * Q, Q * TZ)


def y_tables():
    product = (frequencies(KY)[:, None] * np.arange(NY)[None]) % NY
    angle = product * (2.0 * np.pi / NY)
    cos, sin = np.cos(angle), np.sin(angle)
    full = np.stack([np.stack([cos, sin]), np.stack([-sin, cos])])
    full = full.reshape(2, 2, KY, N_GY, Y).transpose(3, 0, 2, 1, 4)
    return full.reshape(N_GY, 2 * KY, 2 * Y)


def unit_tables():
    lane = np.arange(128)
    row = np.arange(96)
    expand = (lane[None] // 6 == np.arange(16)[:, None]) & (lane[None] < BLOCK)
    keep = ((row[:, None] // 8) % 6 == lane[None] % 6) & (lane[None] < BLOCK)
    return expand.astype(np.float32), keep.astype(np.float32)


def row_matrix(slab):
    shape = (N_Y * ROWS, ROWS)
    row = lax.broadcasted_iota(jnp.int32, shape, 0)
    col = lax.broadcasted_iota(jnp.int32, shape, 1)
    part, part_in = (row % 72) // 36, (col % 24) // 12
    kx = (row // 72) * 3 + (row % 36) // 12
    freq = jnp.where(kx < KX // 2, kx, kx - KX)
    product = (freq * (slab * CX + col // 24)) % NX
    phase = product.astype(F32) * (2.0 * math.pi / NX)
    cos, sin = jnp.cos(phase), jnp.sin(phase)
    value = jnp.where(part == part_in, cos, jnp.where(part == 0, sin, -sin))
    return jnp.where(row % 12 == col % 12, value, 0.0) * FORWARD_SCALE


def dot(a, b, dims, precision=None):
    return lax.dot_general(a, b, (dims, ((), ())), precision=precision, preferred_element_type=F32)


NN = ((1,), (0,))
NT_DIMS = ((1,), (1,))
TN = ((0,), (0,))


def to_pieces(field_ref, depth_ref, y_ref, gy, gsend):
    table = y_ref[gy]
    for x in range(CX):
        for pair in range(2):
            blocks = [
                field_ref[(2 * pair + h) * Q : (2 * pair + h + 1) * Q, x].reshape(Q * TZ, Y)
                for h in range(2)
            ]
            z = dot(depth_ref[...], jnp.concatenate(blocks, axis=1), NN)
            for h in range(2):
                part = z[:, h * Y : (h + 1) * Y]
                both = jnp.concatenate([part[:LANES], part[LANES:]], axis=1).astype(BF16)
                gsend[2 * pair + h, x * 24 : (x + 1) * 24, 0:LANES] = dot(table, both, NT_DIMS)


def comm_kernel(backward, *refs):
    field_ref, depth_ref, y_ref, rows_ref, w_ref, expand_ref, keep_ref = refs[:7]
    if backward:
        modes_ref, local_ref, hall_out, gs_ref, gl_ref = refs[7:12]
        refs = refs[12:]
    else:
        hall_out, modes_out = refs[7:9]
        refs = refs[9:]
    (gsend, grecv, fsend, frecv, units, msend, mrecv, qsend, qbuf, rsend, rall, fall, hsend, hall) = refs[:14]
    sems = refs[14:]

    slab, gy = lax.axis_index("slab"), lax.axis_index("gy")
    yy, rr = lax.div(slab, N_R), lax.rem(slab, N_R)

    def gy_at(d):
        index = lax.rem(gy + d, N_GY)
        return index, {"gy": index}

    def y_at(d):
        index = lax.rem(yy + d, N_Y)
        return index, {"slab": index * N_R + rr}

    def r_at(d):
        index = lax.rem(rr + d, N_R)
        return index, {"slab": yy * N_R + index}

    barrier = pltpu.get_barrier_semaphore()
    for n, at in ((N_GY, gy_at), (N_Y, y_at), (N_R, r_at)):
        for d in range(1, n):
            pl.semaphore_signal(barrier, inc=1, device_id=at(d)[1], device_id_type=MESH)

    started = []

    def send_all(round_index, n, at, source, target):
        send_sem, recv_sem = sems[2 * round_index], sems[2 * round_index + 1]
        copies = []
        for d in range(1, n):
            index, device = at(d)
            copy = pltpu.make_async_remote_copy(
                src_ref=source(index),
                dst_ref=target(d),
                send_sem=send_sem.at[d - 1],
                recv_sem=recv_sem.at[d - 1],
                device_id=device,
                device_id_type=MESH,
            )
            copy.start()
            copies.append(copy)
        for copy in copies:
            copy.wait_recv()
        started.extend(copies)

    to_pieces(field_ref, depth_ref, y_ref, gy, gsend)
    msend[...] = jnp.zeros_like(msend)
    qsend[...] = jnp.zeros_like(qsend)
    rsend[...] = jnp.zeros_like(rsend)
    if backward:
        local = local_ref[...]
        for q in range(N_GY):
            for a in range(2):
                gsend[q, 8 * a : 8 * a + 8, 192:224] = local[16 * a : 16 * a + 8]
                gsend[q, 8 * a : 8 * a + 8, 224:256] = local[16 * a + 8 : 16 * a + 16]
    pl.semaphore_wait(barrier, N_GY + N_Y + N_R - 3)

    send_all(0, N_GY, gy_at, lambda i: gsend.at[i], lambda d: grecv.at[d - 1])
    g = gsend[gy] + grecv[0] + grecv[1] + grecv[2]

    f = dot(rows_ref[...], g[:, 0:LANES], NN, HIGHEST)
    for j in range(N_Y):
        fsend[j, :, 0:LANES] = f[j * ROWS : (j + 1) * ROWS]
        if backward:
            fsend[j, 0:16, LANES:256] = g[0:16, LANES:256]
    send_all(1, N_Y, y_at, lambda i: fsend.at[i], lambda d: frecv.at[d - 1])
    f = fsend[yy] + frecv[0] + frecv[1] + frecv[2]

    blank = jnp.zeros((36, 32), F32)
    for kq in range(4):
        lanes = slice(kq * 48, kq * 48 + 48)
        units[pl.ds(kq, 36, stride=4), :] = jnp.concatenate([f[0:36, lanes], f[36:72, lanes], blank], axis=1)
    for j in range(N_R):
        msend[j, 0:UNITS, :] = units[j * UNITS : (j + 1) * UNITS, :]
        if backward:
            msend[j, 16:24, 0:64] = f[0:8, LANES:256]
            msend[j, 16:24, 64:128] = f[8:16, LANES:256]
    send_all(2, N_R, r_at, lambda i: msend.at[i], lambda d: mrecv.at[d - 1])
    m = msend[rr]
    for d in range(1, N_R):
        m = m + mrecv[d - 1]

    spread = dot(m[0:16, 0:96], expand_ref[...], TN, HIGHEST) * keep_ref[...]
    parts = []
    for part in range(2):
        total = spread[part * 48 : part * 48 + 8]
        for j in range(1, 6):
            total = total + spread[part * 48 + 8 * j : part * 48 + 8 * j + 8]
        parts.append(total)

    if backward:
        for a in range(4):
            gl_ref[8 * a : 8 * a + 8, :] = m[16:24, 32 * a : 32 * a + 32] * FORWARD_SCALE
        gr, gi = parts[0][:, 0:BLOCK], parts[1][:, 0:BLOCK]
        for i in range(C):
            q, c = divmod(i, Q)
            mr, mi = modes_ref[q, c : c + 1, 0:BLOCK], modes_ref[q, 8 + c : 9 + c, 0:BLOCK]
            gs_ref[0, i] = mr * gr + mi * gi
            gs_ref[1, i] = mr * gi - mi * gr
            w0, w1 = w_ref[0, i].astype(F32), w_ref[1, i].astype(F32)
            qsend[q, c : c + 1, 0:BLOCK] = jnp.sum(gr * w0 + gi * w1, axis=0, keepdims=True)
            qsend[q, 8 + c : 9 + c, 0:BLOCK] = jnp.sum(gi * w0 - gr * w1, axis=0, keepdims=True)
        send_all(3, N_GY, gy_at, lambda i: qsend.at[i], lambda d: qbuf.at[d - 1])
        mixed = qsend[gy] + qbuf[0] + qbuf[1] + qbuf[2]
        mixed = [mixed[0:8], mixed[8:16]]
    else:
        qsend[...] = jnp.concatenate(parts, axis=0)
        qbuf[gy] = qsend[...]
        send_all(3, N_GY, gy_at, lambda i: qsend, lambda d: qbuf.at[gy])
        modes_out[...] = qbuf[...]
        mixed_r = jnp.zeros((Q, BLOCK), F32)
        mixed_i = jnp.zeros((Q, BLOCK), F32)
        for i in range(C):
            q, c = divmod(i, Q)
            mr, mi = qbuf[q, c : c + 1, 0:BLOCK], qbuf[q, 8 + c : 9 + c, 0:BLOCK]
            w0, w1 = w_ref[0, i].astype(F32), w_ref[1, i].astype(F32)
            mixed_r = mixed_r + (mr * w0 - mi * w1)
            mixed_i = mixed_i + (mr * w1 + mi * w0)
        pad = jnp.zeros((Q, 128 - BLOCK), F32)
        mixed = [jnp.concatenate([v, pad], axis=1) for v in (mixed_r, mixed_i)]

    tiled = jnp.concatenate([mixed[0]] * 6 + [mixed[1]] * 6, axis=0) * keep_ref[...]
    rsend[:, 0:96] = dot(expand_ref[...], tiled, NT_DIMS, HIGHEST)
    rall[rr] = rsend[...]
    send_all(4, N_R, r_at, lambda i: rsend, lambda d: rall.at[rr])
    for j in range(N_R):
        units[j * UNITS : (j + 1) * UNITS, :] = rall[j, 0:UNITS, :]

    for kq in range(4):
        both = units[pl.ds(kq, 36, stride=4), :]
        for part in range(2):
            fall[yy, part * 36 : part * 36 + 36, kq * 48 : kq * 48 + 48] = both[:, part * 48 : part * 48 + 48]
    send_all(5, N_Y, y_at, lambda i: fall.at[yy], lambda d: fall.at[yy])

    h = dot(rows_ref[...], fall[...].reshape(N_Y * ROWS, 256)[:, 0:LANES], TN, HIGHEST)
    hsend[:, 0:LANES] = h * (INVERSE_SCALE / FORWARD_SCALE)
    hall[gy] = hsend[...]
    send_all(6, N_GY, gy_at, lambda i: hsend, lambda d: hall.at[gy])
    hall_out[...] = hall[...]
    for copy in started:
        copy.wait_send()


def vmem():
    return pl.BlockSpec(memory_space=pltpu.VMEM)


def comm_call(backward, *operands):
    message = 24 if backward else 16
    outs = [jax.ShapeDtypeStruct((N_GY, ROWS, 256), F32)]
    if backward:
        outs.append(jax.ShapeDtypeStruct((2, C, Q, BLOCK), F32))
        outs.append(jax.ShapeDtypeStruct((C, C), F32))
    else:
        outs.append(jax.ShapeDtypeStruct((N_GY, 16, 128), F32))
    big, small = (ROWS, 256), (16, 128)
    shapes = [
        (N_GY, *big),
        (N_GY - 1, *big),
        (N_Y, *big),
        (N_Y - 1, *big),
        (N_R * UNITS, 128),
        (N_R, message, 128),
        (N_R - 1, message, 128),
        (N_GY, *small) if backward else small,
        (N_GY - 1, *small) if backward else (N_GY, *small),
        small,
        (N_R, *small),
        (N_Y, *big),
        big,
        (N_GY, *big),
    ]
    scratch = [pltpu.VMEM(shape, F32) for shape in shapes]
    for n in (N_GY, N_Y, N_R, N_GY, N_R, N_Y, N_GY):
        scratch += [pltpu.SemaphoreType.DMA((n - 1,))] * 2
    return pl.pallas_call(
        functools.partial(comm_kernel, backward),
        out_shape=outs,
        in_specs=[vmem() for _ in operands],
        out_specs=[vmem() for _ in outs],
        scratch_shapes=scratch,
        compiler_params=pltpu.CompilerParams(
            collective_id=1 if backward else 0,
            has_side_effects=True,
            vmem_limit_bytes=32 * 1024 * 1024,
        ),
        name="modes_backward" if backward else "modes_forward",
    )(*operands)


def spectral_rows(hall_ref, y_ref, depth_ref, gy, x, spec):
    for pair in range(2):
        halves = []
        for q in (2 * pair, 2 * pair + 1):
            h = hall_ref[q, pl.ds(pl.multiple_of(x * 24, 8), 24), 0:LANES]
            high = h.astype(BF16).astype(F32)
            stacked = jnp.concatenate([high, high, h - high], axis=0).astype(BF16)
            u = dot(stacked, y_ref[gy], TN)
            halves.append(jnp.concatenate([u[:, :Y], u[:, Y:]], axis=0).astype(BF16))
        s = dot(depth_ref[...], jnp.concatenate(halves, axis=1), NN)
        for h in range(2):
            q = 2 * pair + h
            spec[q * Q : (q + 1) * Q] = s[:, h * Y : (h + 1) * Y].reshape(Q, TZ, Y)


def chunk_of(ref, r):
    values = ref[:, r * 16 : (r + 1) * 16, :].astype(F32)
    return jnp.concatenate([values[:, 0:8].reshape(256, Y), values[:, 8:16].reshape(256, Y)], axis=1)


def unchunk(values):
    halves = [values[:, :Y].reshape(C, 8, Y), values[:, Y:].reshape(C, 8, Y)]
    return jnp.concatenate(halves, axis=1)


def channel_matrix(weight, repeat_ref, transposed):
    repeat = repeat_ref[...]
    half = dot(repeat, weight, NT_DIMS if transposed else NN).astype(BF16)
    full = dot(half, repeat, NT_DIMS)
    row = lax.broadcasted_iota(jnp.int32, full.shape, 0)
    col = lax.broadcasted_iota(jnp.int32, full.shape, 1)
    return jnp.where(row % 8 == col % 8, full, 0.0).astype(BF16)


def forward_kernel(field_ref, cot_ref, hall_ref, y_ref, depth_ref, lw_ref, repeat_ref, out_ref, grad_ref, local_ref, spec, acc, kron):
    x, gy = pl.program_id(0), lax.axis_index("gy")

    @pl.when(x == 0)
    def _():
        kron[...] = channel_matrix(lw_ref[...], repeat_ref, True)
        acc[...] = jnp.zeros_like(acc)

    spectral_rows(hall_ref, y_ref, depth_ref, gy, x, spec)
    for r in range(TZ // 16):
        cells = chunk_of(field_ref.at[:, 0], r).astype(BF16)
        pre = chunk_of(spec, r) + dot(kron[...], cells, NN)
        cdf = 0.5 * (1.0 + lax.erf(pre * ROOT_HALF))
        slope = cdf + pre * jnp.exp(-0.5 * pre * pre) * INV_ROOT_TWO_PI
        grad = chunk_of(cot_ref.at[:, 0], r) * slope
        out_ref[:, 0, r * 16 : (r + 1) * 16, :] = unchunk(pre * cdf).astype(BF16)
        grad_ref[:, 0, r * 16 : (r + 1) * 16, :] = unchunk(grad).astype(BF16)
        acc[...] += dot(cells, grad.astype(BF16), NT_DIMS)

    @pl.when(x == CX - 1)
    def _():
        row = lax.broadcasted_iota(jnp.int32, acc.shape, 0)
        col = lax.broadcasted_iota(jnp.int32, acc.shape, 1)
        kept = jnp.where(row % 8 == col % 8, acc[...], 0.0)
        repeat = repeat_ref[...].astype(F32)
        local_ref[...] = dot(dot(repeat, kept, TN, HIGHEST), repeat, NN, HIGHEST)


def backward_kernel(grad_ref, hall_ref, y_ref, depth_ref, lw_ref, repeat_ref, out_ref, spec, kron):
    x, gy = pl.program_id(0), lax.axis_index("gy")

    @pl.when(x == 0)
    def _():
        kron[...] = channel_matrix(lw_ref[...], repeat_ref, False)

    spectral_rows(hall_ref, y_ref, depth_ref, gy, x, spec)
    for r in range(TZ // 16):
        cells = chunk_of(grad_ref.at[:, 0], r).astype(BF16)
        total = chunk_of(spec, r) + dot(kron[...], cells, NN)
        out_ref[:, 0, r * 16 : (r + 1) * 16, :] = unchunk(total).astype(BF16)


def row_spec():
    return pl.BlockSpec((C, 1, TZ, Y), lambda x: (0, x, 0, 0))


def per_device(field_in, cotangent, spectral_weight, local_weight):
    cells = (C, CX, TZ, Y)
    field = field_in.reshape(cells)
    cot = cotangent.reshape(cells)
    weight = jnp.transpose(spectral_weight, (0, 2, 3, 1))
    depth = depth_table()
    tables = y_tables()
    high = tables.astype(BF16)
    low = (tables - high.astype(np.float64)).astype(BF16)
    depth_forward = jnp.asarray(depth.astype(BF16))
    depth_back = jnp.asarray(np.ascontiguousarray(depth.T).astype(BF16))
    y_forward = jnp.asarray(high)
    y_back = jnp.asarray(np.concatenate([high, low, high], axis=1))
    expand, keep = unit_tables()
    expand, keep = jnp.asarray(expand), jnp.asarray(keep)
    repeat = jnp.asarray(np.repeat(np.eye(C), 8, axis=0).astype(BF16))
    rows = row_matrix(lax.axis_index("slab"))

    hall, modes = comm_call(False, field, depth_forward, y_forward, rows, weight, expand, keep)
    field_shape = jax.ShapeDtypeStruct(cells, BF16)
    params = pltpu.CompilerParams(vmem_limit_bytes=32 * 1024 * 1024)
    output, grad_pre, local_terms = pl.pallas_call(
        forward_kernel,
        grid=(CX,),
        out_shape=[field_shape, field_shape, jax.ShapeDtypeStruct((C, C), F32)],
        in_specs=[row_spec(), row_spec()] + [vmem()] * 5,
        out_specs=[row_spec(), row_spec(), pl.BlockSpec((C, C), lambda x: (0, 0))],
        scratch_shapes=[pltpu.VMEM((C, TZ, Y), F32), pltpu.VMEM((256, 256), F32), pltpu.VMEM((256, 256), BF16)],
        compiler_params=params,
        name="cells_forward",
    )(field, cot, hall, y_back, depth_back, local_weight, repeat)
    hall, grad_spectral, grad_local = comm_call(
        True, grad_pre, depth_forward, y_forward, rows, weight, expand, keep, modes, local_terms
    )
    grad_input = pl.pallas_call(
        backward_kernel,
        grid=(CX,),
        out_shape=field_shape,
        in_specs=[row_spec()] + [vmem()] * 5,
        out_specs=row_spec(),
        scratch_shapes=[pltpu.VMEM((C, TZ, Y), F32), pltpu.VMEM((256, 256), BF16)],
        compiler_params=params,
        name="cells_backward",
    )(grad_pre, hall, y_back, depth_back, local_weight, repeat)
    return (
        output.reshape(field_in.shape),
        grad_input.reshape(field_in.shape),
        jnp.transpose(grad_spectral, (0, 3, 1, 2)),
        grad_local,
    )


def solution(mesh):
    placed = (
        P(None, "slab", None, None, "gy"),
        P(None, "slab", None, None, "gy"),
        P(None, "slab", None, "gy"),
        P(),
    )
    return jax.shard_map(
        per_device,
        mesh=mesh,
        in_specs=placed,
        out_specs=(
            P(None, "slab", None, None, "gy"),
            P(None, "slab", None, None, "gy"),
            P(None, "slab", None, "gy"),
            P(),
        ),
        check_vma=False,
    )
```

time: 1450 us -> 116 us (0.08)
  blocking collectives: 1160 us -> 0 us
  starting transfers between devices: 124 us -> 0 us
  Pallas kernels: 0 us -> 106 us
  matrix products: 87.6 us -> 0 us
  local copies, waits for them, and re-layouts: 59.7 us -> 6.93 us
    all_gather x8 -> x0, blocking collectives: 660 us -> none  [the longest x2 260 us: from_modes(): lax.all_gather(spectrum[0], 'slab', axis=0, tiled=True)]
    unnamed x3 -> x0, blocking collectives: 328 us -> none
    psum x3 -> x0, blocking collectives: 173 us -> none  [the longest x1 107 us: per_device(): grad_local = lax.psum(local_terms, ('slab', 'gy')) * forward_scale]
    unnamed x40 -> x0, starting transfers between devices: 124 us -> none
    pallas_call x0 -> x4, Pallas kernels: none -> 106 us  [the longest x2 95.9 us: comm_call(): pl.pallas_call(functools.partial(comm_kernel, backward), out_shape=outs,...]
    dot_general x39 -> x0, matrix products: 87.6 us -> none  [the longest x8 20.3 us: rows_forward(): return jnp.einsum('crkq,rp->pkqc', values, table, precision=highest)]
    unnamed x112 -> x26, local copies, waits for them, and re-layouts: 46.6 us -> 6.93 us
  transfers between devices with their start and end apart: 40 -> 0, of which waited for: 1 -> 0; matrix products, arithmetic and copies ran while one was open for 3% -> 0% of each run, Pallas kernels for 0% -> 0%
where the time goes in v1:
time: 116 us
  Pallas kernels  106 us (91%)
  local copies, waits for them, and re-layouts  6.93 us (6%)
  other arithmetic  1.81 us (2%)
    pallas_call x2, Pallas kernels, comm_call(): pl.pallas_call(functools.partial(comm_kernel, backward), out_shape=outs,...  95.9 us
    unnamed x26, local copies, waits for them, and re-layouts  6.93 us
    pallas_call x1, Pallas kernels, per_device(): pl.pallas_call(forward_kernel, grid=(CX,), out_shape=[field_shape, field_...  6.35 us
    pallas_call x1, Pallas kernels, per_device(): pl.pallas_call(backward_kernel, grid=(CX,), out_shape=field_shape, in_spe...  3.84 us

profile of v1, /device:TPU:1, one launch (start us, length us, event | category | flops | bytes accessed | tf_op | source)
XLA Modules:
  0.0 115.6 jit_solution(15309694264876296998)
XLA Ops:
  0.6 0.0 copy-start.7
  0.6 0.0 copy-start.5
  0.7 0.0 copy-start.10
  0.8 1.7 %fusion.6.refs_3_ = f32[288,72]{1,0:T(8,128)S(1)} fusion(s32[72]{0:T(128)S(1)} %get-tuple-element.34, s32[72]{0:T(128)S(1)} %get-tuple-element.37, s32[]{:T(128)S(6)} %mul.26, s32[288]{0:T(512)S(1)} %get-tuple-element.20, s32[288]{0:T(512)S(1)} %get-tuple-element.22, s32[288]{0:T(512)S(1)} %get-tuple-element.21, s32[288]{0:T(512)S(1)} %get-tuple-element.27, ...), kind=kLoop, calls=%fused_computation.21 | loop fusion | flops 1119744 | bytes 95260 | tf_op jit(solution)/shard_map/mul | solution.py:86
  2.5 0.0 copy-start
  2.6 1.4 %copy-done = bf16[32,3,2,32,128]{4,3,2,1,0:T(8,128)(2,1)S(1)} copy-done((bf16[32,3,2,32,128]{4,3,2,1,0:T(8,128)(2,1)S(1)}, bf16[32,3,2,32,128]{4,3,2,1,0:T(8,128)(2,1)}, u32[]{:S(2)}) %copy-start) | copy-done | bytes 1572888
  4.0 0.0 copy-start.1
  4.0 1.0 copy-done.1
  4.9 0.0 copy-start.6
  5.0 0.9 copy-done.6
  5.9 0.0 copy-start.8
  5.9 0.8 copy-done.8
  6.7 0.0 copy-start.9
  6.7 0.8 copy-done.9
  7.5 0.0 copy-start.11
  7.5 0.7 copy-done.11
  8.1 0.0 copy-start.3
  8.2 0.0 copy-start.4
  8.2 51.4 %modes_forward.1 = (f32[4,72,256]{2,1,0:T(8,128)S(1)}, f32[4,16,128]{2,1,0:T(8,128)S(1)}) custom-call(bf16[32,3,64,128]{3,2,1,0:T(8,128)(2,1)S(1)} %bitcast.6, bf16[384,512]{1,0:T(8,128)(2,1)S(1)} %copy-done.1, bf16[4,24,256]{2,1,0:T(8,128)(2,1)S(1)} %copy-done.9, f32[288,72]{1,0:T(8,128)S(1)} %fusion.6.refs_3_, bf16[2,32,8,54]{3,2,1,0:T(8,128)(2,1)S(1)} %bitcast.9, ...), custom_call_target="tpu_custom_call" | custom-call | tf_op jit(solution)/shard_map/modes_forward/pallas_call | solution.py:295
  59.6 0.0 copy-done.7
  59.6 0.0 copy-done.5
  59.6 0.0 copy-done.10
  59.6 0.0 copy-done.3
  59.6 0.0 copy-done.4
  59.6 0.0 copy-start.2
  59.7 6.3 %cells_forward.1 = (bf16[32,3,64,128]{3,2,1,0:T(8,128)(2,1)}, bf16[32,3,64,128]{3,2,1,0:T(8,128)(2,1)S(1)}, f32[32,32]{1,0:T(8,128)S(1)}) custom-call(bf16[32,3,64,128]{3,2,1,0:T(8,128)(2,1)S(1)} %bitcast.7, bf16[32,3,64,128]{3,2,1,0:T(8,128)(2,1)S(1)} %bitcast.8, f32[4,72,256]{2,1,0:T(8,128)S(1)} %get-tuple-element.12.hall_ref, ...), custom_call_target="tpu_custom_call" | custom-call | tf_op jit(solution)/shard_map/cells_forward/pallas_call | solution.py:411
  66.0 0.0 copy-done.2
  66.0 44.5 %modes_backward.1 = (f32[4,72,256]{2,1,0:T(8,128)S(1)}, f32[2,32,8,54]{3,2,1,0:T(8,128)S(1)}, f32[32,32]{1,0:T(8,128)S(1)}) custom-call(bf16[32,3,64,128]{3,2,1,0:T(8,128)(2,1)S(1)} %get-tuple-element.14.refs_0_.grad_ref, bf16[384,512]{1,0:T(8,128)(2,1)S(1)} %copy-done.2, bf16[4,24,256]{2,1,0:T(8,128)(2,1)S(1)} %copy-done.9, f32[288,72]{1,0:T(8,128)S(1)} %fusion.6.refs_3_, ...), custom_call_target="tpu_custom_call" | custom-call | tf_op jit(solution)/shard_map/modes_backward/pallas_call | solution.py:295
  110.5 3.8 %cells_backward.1 = bf16[32,3,64,128]{3,2,1,0:T(8,128)(2,1)} custom-call(bf16[32,3,64,128]{3,2,1,0:T(8,128)(2,1)S(1)} %get-tuple-element.14.refs_0_.grad_ref, f32[4,72,256]{2,1,0:T(8,128)S(1)} %get-tuple-element.17.hall_ref, bf16[4,72,256]{2,1,0:T(8,128)(2,1)S(1)} %copy-done.5, bf16[512,384]{1,0:T(8,128)(2,1)S(1)} %copy-done.4, ...), custom_call_target="tpu_custom_call" | custom-call | tf_op jit(solution)/shard_map/cells_backward/pallas_call | solution.py:424
  114.3 0.7 copy.17
  115.0 0.6 copy.18
  (11 shorter events, 0.1 us)
Async XLA Ops:
  0.6 59.0 %copy-start.7 = (bf16[256,32]{1,0:T(8,128)(2,1)S(1)}, bf16[256,32]{1,0:T(8,128)(2,1)}, u32[]{:S(2)}) copy-start(bf16[256,32]{1,0:T(8,128)(2,1)} %constant.111.clone.repeat_ref) | copy-start | bytes 49156
  0.6 59.0 %copy-start.5 = (bf16[4,72,256]{2,1,0:T(8,128)(2,1)S(1)}, bf16[4,72,256]{2,1,0:T(8,128)(2,1)}, u32[]{:S(2)}) copy-start(bf16[4,72,256]{2,1,0:T(8,128)(2,1)} %constant.108.clone.y_ref) | copy-start | bytes 442372
  0.7 59.0 %copy-start.10 = (bf16[32,32]{1,0:T(8,128)(2,1)S(1)}, bf16[32,32]{1,0:T(8,128)(2,1)}, u32[]{:S(2)}) copy-start(bf16[32,32]{1,0:T(8,128)(2,1)} %lw_ref.3) | copy-start | bytes 6148
  2.5 1.4 %copy-start = (bf16[32,3,2,32,128]{4,3,2,1,0:T(8,128)(2,1)S(1)}, bf16[32,3,2,32,128]{4,3,2,1,0:T(8,128)(2,1)}, u32[]{:S(2)}) copy-start(bf16[32,3,2,32,128]{4,3,2,1,0:T(8,128)(2,1)} %param.11) | copy-start | bytes 4718596
  4.0 1.0 copy-start.1
  4.9 0.9 copy-start.6
  5.9 0.8 copy-start.8
  6.7 0.8 copy-start.9
  7.5 0.7 copy-start.11
  8.1 51.5 %copy-start.3 = (bf16[32,3,2,32,128]{4,3,2,1,0:T(8,128)(2,1)S(1)}, bf16[32,3,2,32,128]{4,3,2,1,0:T(8,128)(2,1)}, u32[]{:S(2)}) copy-start(bf16[32,3,2,32,128]{4,3,2,1,0:T(8,128)(2,1)} %param.12) | copy-start | bytes 4718596
  8.2 51.5 %copy-start.4 = (bf16[512,384]{1,0:T(8,128)(2,1)S(1)}, bf16[512,384]{1,0:T(8,128)(2,1)}, u32[]{:S(2)}) copy-start(bf16[512,384]{1,0:T(8,128)(2,1)} %constant.106.clone.depth_ref) | copy-start | bytes 1179652
  59.6 6.4 %copy-start.2 = (bf16[384,512]{1,0:T(8,128)(2,1)S(1)}, bf16[384,512]{1,0:T(8,128)(2,1)}, u32[]{:S(2)}) copy-start(bf16[384,512]{1,0:T(8,128)(2,1)} %constant.105.clone.refs_1_) | copy-start | bytes 1179652

commit v2 on v1

v2 whole, which is shorter than its diff:
```python
import functools
import math

import jax
import jax.numpy as jnp
import numpy as np
from jax import lax
from jax.experimental import pallas as pl
from jax.experimental.pallas import tpu as pltpu
from jax.sharding import PartitionSpec as P

C = 32
KX = 12
KY = 12
KZ = 12
NT = 2
NZ = 32
NX = 192
NY = 512
CX = 3
N_GY = 4
N_Y = 4
N_R = 16
Q = C // N_GY
K = NT * KZ
TZ = NT * NZ
Y = NY // N_GY
BLOCK = 54
UNITS = 9
ROWS = 72
LANES = K * Q

FORWARD_SCALE = 1.0 / math.sqrt(NX * NY * NZ * NT)
INVERSE_SCALE = 1.0 / math.sqrt(KX * KY * KZ * NT)
ROOT_HALF = 0.7071067811865476
INV_ROOT_TWO_PI = 0.3989422804014327
HIGHEST = lax.Precision.HIGHEST
WINDOW = [(z % 4) * 4 + x * 2 + z // 4 for x in range(2) for z in range(8)]
PLANE = [(h, c, y) for h in range(2) for c in range(2) for y in range(N_Y) if (h, c, y) != (0, 0, 0)]
PLANE.sort(key=lambda d: -(2 * d[0] + min(d[2], N_Y - d[2])))
COLUMN = [(x, z) for x in range(2) for z in range(8) if (x, z) != (0, 0)]
COLUMN.sort(key=lambda d: -(d[0] + min(d[1], 8 - d[1])))
QUARTER = [(1, 1), (1, 0), (0, 1)]
F32 = jnp.float32
BF16 = jnp.bfloat16
MESH = pl.DeviceIdType.MESH


def frequencies(kept):
    values = np.arange(kept)
    return np.where(values < kept // 2, values, values - kept)


def depth_table():
    t, z = np.divmod(np.arange(TZ), NZ)
    kt, kz = np.divmod(np.arange(K), KZ)
    product = (t[None] * kt[:, None] * NZ + z[None] * frequencies(KZ)[kz][:, None] * NT) % TZ
    angle = product * (2.0 * np.pi / TZ)
    parts = np.stack([np.cos(angle), -np.sin(angle)])
    full = np.einsum("pks,cd->pkcds", parts, np.eye(Q))
    return full.reshape(2 * K * Q, Q * TZ)


def y_tables():
    product = (frequencies(KY)[:, None] * np.arange(NY)[None]) % NY
    angle = product * (2.0 * np.pi / NY)
    cos, sin = np.cos(angle), np.sin(angle)
    full = np.stack([np.stack([cos, sin]), np.stack([-sin, cos])])
    full = full.reshape(2, 2, KY, N_GY, Y).transpose(3, 0, 2, 1, 4)
    return full.reshape(N_GY, 2 * KY, 2 * Y)


def unit_tables():
    lane = np.arange(128)
    row = np.arange(96)
    expand = (lane[None] // 6 == np.arange(16)[:, None]) & (lane[None] < BLOCK)
    keep = ((row[:, None] // 8) % 6 == lane[None] % 6) & (lane[None] < BLOCK)
    return expand.astype(np.float32), keep.astype(np.float32)


def row_tables():
    main = [9 * w + j for w in WINDOW for j in range(8)]
    ninth = [9 * w + 8 for w in WINDOW]
    pairs = np.array(main + main + ninth + ninth)
    part = np.array([0] * 128 + [1] * 128 + [0] * 16 + [1] * 16)
    y, x, part_in, ky = np.unravel_index(np.arange(288), (N_Y, CX, 2, KY))
    row = 48 * y[None] + 3 * np.arange(N_R)[:, None] + x[None]
    freq = frequencies(KX)[pairs // KY]
    angle = (freq[None, :, None] * row[:, None, :]) % NX * (2.0 * np.pi / NX)
    sign = np.where(part == 0, 1.0, -1.0)[:, None]
    value = np.where(part[:, None] == part_in[None], np.cos(angle), sign * np.sin(angle))
    value = np.where((pairs % KY)[:, None] == ky[None], value, 0.0)
    forward, inverse = value * FORWARD_SCALE, value.transpose(0, 2, 1) * INVERSE_SCALE
    parts = []
    for full in (forward, inverse):
        high = full.astype(BF16)
        parts += [high, (full - high.astype(np.float64)).astype(BF16)]
    return np.stack(parts, axis=1)


def owner_tables():
    select = np.zeros((4, 72, 128))
    place = np.zeros((4, 2, 72, 128))
    gather = np.zeros((4, 4, 128, 128))
    for t in range(4):
        count = [0] * 4
        for mode in range(BLOCK):
            unit = 9 * t + mode // 6
            y, other = unit % 4, 6 * (unit // 4) + mode % 6
            n = count[y]
            count[y] += 1
            if n < 12:
                select[t, 16 * y + n, mode] = 1.0
            else:
                select[t, 64 + n - 12, mode] = 1.0
            for half in range(2):
                row = 8 * t + n if n < 8 else 40 + 8 * t + 4 * half + n - 8 if n < 12 else 32 + n - 12
                place[y, half, row, other] = 1.0
            for part in range(2):
                gather[t, y, part * BLOCK + other, part * BLOCK + mode] = 1.0
    return select, place.reshape(4, 144, 128), gather.reshape(4, 512, 128)


def dot(a, b, dims, precision=None):
    return lax.dot_general(a, b, (dims, ((), ())), precision=precision, preferred_element_type=F32)


NN = ((1,), (0,))
NT_DIMS = ((1,), (1,))
TN = ((0,), (0,))


def comm_kernel(backward, *refs):
    field_ref, depth_hbm, y_hbm, rows_hbm, expand_hbm, keep_hbm, gather_hbm = refs[:7]
    if backward:
        owned_ref, modes_ref, local_ref, hall_out, gs_ref, gl_ref = refs[7:13]
        refs = refs[13:]
    else:
        w_hbm, select_hbm, place_hbm, hall_out, modes_out, owned_out = refs[7:13]
        refs = refs[13:]
    (depth_ref, y_ref, rows_ref, expand_ref, keep_ref, gather_ref) = refs[:6]
    (z_all, gsend, grecv, g12, msend, mrecv, qsend, qbuf, rows8, rsend, rall, hsend, hall, l1buf) = refs[6:20]
    load_sem, *sems = refs[20:28]
    if not backward:
        w_ref, select_ref, place_ref, wsend, wrecv, third_unit, third_sem, field_vmem, field_sem = refs[28:]

    slab, gy = lax.axis_index("slab"), lax.axis_index("gy")
    yy, rr = lax.div(slab, N_R), lax.rem(slab, N_R)
    x_hi, core = lax.div(gy, 2), lax.rem(gy, 2)
    x_lo, z = lax.div(rr, 8), lax.rem(rr, 8)
    turn, half = lax.rem(z, 4), lax.div(z, 4)

    staged = [
        (depth_hbm, depth_ref),
        (y_hbm.at[gy], y_ref),
        (rows_hbm.at[rr], rows_ref),
        (expand_hbm, expand_ref),
        (keep_hbm, keep_ref),
        (gather_hbm.at[turn], gather_ref),
    ]
    if not backward:
        staged += [(w_hbm, w_ref), (select_hbm.at[turn], select_ref), (place_hbm.at[yy], place_ref)]
    loads = [pltpu.make_async_copy(a, b, load_sem.at[k]) for k, (a, b) in enumerate(staged)]
    if not backward:
        pieces = [
            pltpu.make_async_copy(field_ref.at[:, x], field_vmem.at[x], field_sem.at[x]) for x in range(CX)
        ]
        pieces[0].start()
    for load in loads:
        load.start()
    if not backward:
        pieces[1].start()
        pieces[2].start()

    def plane(k):
        d_hi, d_core, dy = PLANE[k]
        g_to = lax.rem(x_hi + d_hi, 2) * 2 + lax.rem(core + d_core, 2)
        y_to = lax.rem(yy + dy, N_Y)
        return g_to, y_to, {"gy": g_to, "slab": y_to * N_R + rr}

    def column(k):
        d_lo, dz = COLUMN[k]
        r_to = lax.rem(x_lo + d_lo, 2) * 8 + lax.rem(z + dz, 8)
        return r_to, {"slab": yy * N_R + r_to}

    def quarter(k):
        d_hi, d_core = QUARTER[k]
        g_to = lax.rem(x_hi + d_hi, 2) * 2 + lax.rem(core + d_core, 2)
        return g_to, {"gy": g_to}

    owners = [k * N_R + x_lo * 8 + half * 4 + yy for k in range(4)]
    blocks = [turn * N_R + x_lo * 8 + half * 4 + k for k in range(4)]
    at_home = (turn == yy).astype(jnp.int32)

    barrier = pltpu.get_barrier_semaphore()

    def greet(device):
        pl.semaphore_signal(barrier, inc=1, device_id=device, device_id_type=MESH)

    for k in range(15):
        greet(plane(k)[2])
        greet(column(k)[1])
    for other in owners + blocks:
        pl.when(other != slab)(functools.partial(greet, {"slab": other}))

    def copy_to(source, target, send_sem, recv_sem, device):
        return pltpu.make_async_remote_copy(
            src_ref=source,
            dst_ref=target,
            send_sem=send_sem,
            recv_sem=recv_sem,
            device_id=device,
            device_id_type=MESH,
        )

    started = []

    def start_all(round_index, copies):
        sem = sems[round_index]
        made = [copy_to(a, b, sem.at[0, k], sem.at[1, k], device) for k, (a, b, device) in enumerate(copies)]
        for copy in made:
            copy.start()
        started.extend(made)
        return made

    def finish(made):
        for copy in made:
            copy.wait_recv()

    def cross(index, buffer, source, target):
        sem = sems[5 + index]
        return [
            (target[k] != slab, copy_to(source(k), buffer, sem.at[0, k], sem.at[1, slot], {"slab": target[k]}))
            for k, slot in ((k, turn if index == 0 else yy) for k in range(4))
        ]

    def start_cross(made):
        for away, copy in made:
            pl.when(away)(copy.start)

    def finish_cross(index, buffer, source, origin):
        sem = sems[5 + index]
        for k in range(4):
            copy = copy_to(source, buffer.at[k], sem.at[0, k], sem.at[1, k], {"slab": origin[k]})
            pl.when(origin[k] != slab)(copy.wait_recv)

    loads[0].wait()
    loads[1].wait()
    table = y_ref[...]
    for x in range(CX):
        if not backward:
            pieces[x].wait()
        for pair in range(2):
            channels = [slice((2 * pair + h) * Q, (2 * pair + h + 1) * Q) for h in range(2)]
            cells = [(field_ref[c, x] if backward else field_vmem[x, c]).reshape(Q * TZ, Y) for c in channels]
            zz = dot(depth_ref[...], jnp.concatenate(cells, axis=1), NN)
            for h in range(2):
                part = zz[:, h * Y : (h + 1) * Y]
                both = jnp.concatenate([part[:LANES], part[LANES:]], axis=1).astype(BF16)
                z_all[2 * pair + h, x] = both
    pl.semaphore_wait(barrier, 30 + 8 - 2 * at_home)
    if not backward:
        for load in loads[6:]:
            load.wait()
        flat = w_ref[...].astype(F32).reshape(2 * C * Q, BLOCK).astype(BF16)
        picked = dot(select_ref[...][:, 0:BLOCK].astype(BF16), flat, NT_DIMS)
        for k in range(4):
            four = picked[16 * k + 8 : 16 * k + 12]
            four = jnp.concatenate([four[:, 0:256], four[:, 256:512]], axis=0)
            wsend[k] = jnp.concatenate([picked[16 * k : 16 * k + 8], four], axis=1)
        third_unit[0] = picked[64:72]
        w_copies = cross(0, wrecv.at[turn], lambda k: wsend.at[k], owners)
        home = turn * N_R + x_lo * 8 + half * 4 + yy
        extra = copy_to(third_unit.at[0], third_unit.at[1], third_sem.at[0], third_sem.at[1], {"slab": home})
        w_copies.append((turn != yy, extra))

        @pl.when(turn == yy)
        def _():
            wrecv[turn] = wsend[yy]
            third_unit[1] = third_unit[0]

    for q in range(N_GY):
        for kq in range(4):
            rows = [z_all[q, x, kq * 48 : kq * 48 + 48, :] for x in range(CX)]
            g = dot(table, jnp.concatenate(rows, axis=0), NT_DIMS)
            tail = [local_ref[8 * q : 8 * q + 8, 8 * kq : 8 * kq + 8]] if backward else []
            gsend[q, kq] = pack(g, tail)

    plane_to = [plane(k) for k in range(15)]
    first = start_all(0, [(gsend.at[g, y], grecv.at[k], device) for k, (g, y, device) in enumerate(plane_to)])
    for load in loads[2:6]:
        load.wait()
    if not backward:
        start_cross(w_copies)
    finish(first)
    slot = {PLANE[k]: k for k in range(15)}
    local = None
    for dy in range(N_Y):
        total = gsend[gy, yy] if dy == 0 else None
        for d_hi in range(2):
            for d_core in range(2):
                if (d_hi, d_core, dy) in slot:
                    term = grecv[slot[d_hi, d_core, dy]]
                    total = term if total is None else total + term
        if backward:
            block = total[24:32, 48:56]
            local = block if local is None else local + block
        base = lax.rem(yy + N_Y - dy, N_Y) * ROWS
        for x, piece in enumerate(unpack(total)):
            g12[pl.ds(pl.multiple_of(base + 24 * x, 8), 24), 0:48] = piece

    f = product(rows_ref, 0, g12[:, 0:48])
    blank = jnp.zeros((128, 24), F32)
    corner = jnp.concatenate([local] * N_R, axis=0) if backward else jnp.zeros((128, 8), F32)
    msend[...] = jnp.concatenate([f[0:128], f[128:256], blank, corner], axis=1)
    ninth = jnp.concatenate([f[256:272], f[272:288]], axis=1)
    for j in range(4):
        old = msend[pl.ds(j, N_R, stride=8), :]
        msend[pl.ds(j, N_R, stride=8), :] = jnp.concatenate(
            [old[:, 0:96], ninth[:, 24 * j : 24 * j + 24], old[:, 120:128]], axis=1
        )

    def window(r):
        return pl.ds(pl.multiple_of(r * 8, 8), 8)

    column_to = [column(k) for k in range(15)]
    second = start_all(1, [(msend.at[window(r)], mrecv.at[k], device) for k, (r, device) in enumerate(column_to)])
    if not backward:
        finish_cross(0, wrecv, wsend.at[0], blocks)
        pl.when(turn != yy)(extra.wait_recv)
        eights = jnp.concatenate([wrecv[t, :, 0:512] for t in range(4)] + [third_unit[1]], axis=0)
        fours = jnp.concatenate([wrecv[t, :, 512:768] for t in range(4)], axis=0)
        for side in range(2):
            lanes = slice(256 * side, 256 * side + 256)
            received = jnp.concatenate([eights[:, lanes], fours], axis=0).astype(BF16)
            owned_out[lanes] = dot(received, place_ref[72 * side : 72 * side + 72, :].astype(BF16), TN)
    finish(second)
    m = msend[window(rr), :]
    for k in range(15):
        m = m + mrecv[k]

    last = jnp.concatenate([m[j : j + 1, 96:120] for j in range(4)], axis=1)
    nine = jnp.concatenate([m[:, 0:96], last, jnp.zeros((7, 96), F32)], axis=0)
    spread = dot(nine, expand_ref[...], TN, HIGHEST) * keep_ref[...]
    parts = []
    for part in range(2):
        total = spread[part * 48 : part * 48 + 8]
        for j in range(1, 6):
            total = total + spread[part * 48 + 8 * j : part * 48 + 8 * j + 8]
        parts.append(total[:, 0:BLOCK])

    def weights(i):
        source = owned_ref if backward else owned_out
        return source[8 * i : 8 * i + 8, 0:BLOCK], source[256 + 8 * i : 264 + 8 * i, 0:BLOCK]

    end = jnp.zeros((Q, 128 - 2 * BLOCK), F32)
    if backward:
        total_local = m[:, 120:128]
        gr, gi = parts
        l1_source = rsend.at[1]
        rsend[1] = jnp.concatenate([gr, gi, end], axis=1)
        for i in range(C):
            q, c = divmod(i, Q)
            w0, w1 = weights(i)
            rows8[q, c : c + 1, 0:BLOCK] = jnp.sum(gr * w0 + gi * w1, axis=0, keepdims=True)
            rows8[q, 8 + c : 9 + c, 0:BLOCK] = jnp.sum(gi * w0 - gr * w1, axis=0, keepdims=True)
        for q in range(N_GY):
            qsend[q] = jnp.concatenate([rows8[q, 0:8, 0:BLOCK], rows8[q, 8:16, 0:BLOCK], end], axis=1)
        third = start_all(2, [(qsend.at[g], qbuf.at[k], device) for k, (g, device) in enumerate(map(quarter, range(3)))])
    else:
        l1_source = qbuf
        qsend[0] = jnp.concatenate([*parts, end], axis=1)
        qbuf[gy] = qsend[0]
        third = start_all(2, [(qsend.at[0], qbuf.at[gy], device) for g, device in map(quarter, range(3))])

    if backward:
        l1_copies = cross(1, l1buf.at[yy], lambda k: l1_source, blocks)
        start_cross(l1_copies)
        finish(third)
        mixed = qsend[gy] + qbuf[0] + qbuf[1] + qbuf[2]
        mixed = [mixed[:, 0:BLOCK], mixed[:, BLOCK : 2 * BLOCK]]
    else:
        finish(third)
        mixed_r = jnp.zeros((Q, BLOCK), F32)
        mixed_i = jnp.zeros((Q, BLOCK), F32)
        for q in range(N_GY):
            real, imag = qbuf[q, :, 0:BLOCK], qbuf[q, :, BLOCK : 2 * BLOCK]
            for c in range(Q):
                mr, mi = real[c : c + 1], imag[c : c + 1]
                w0, w1 = weights(q * Q + c)
                mixed_r = mixed_r + (mr * w0 - mi * w1)
                mixed_i = mixed_i + (mr * w1 + mi * w0)
        mixed = [mixed_r, mixed_i]

    pad = jnp.zeros((Q, 128 - BLOCK), F32)
    mixed = [jnp.concatenate([v, pad], axis=1) for v in mixed]
    tiled = jnp.concatenate([mixed[0]] * 6 + [mixed[1]] * 6, axis=0) * keep_ref[...]
    u = dot(expand_ref[...], tiled, NT_DIMS, HIGHEST)
    last = jnp.concatenate([u[8:9, 24 * j : 24 * j + 24] for j in range(4)] + [jnp.zeros((4, 24), F32)], axis=0)
    rsend[0] = jnp.concatenate([u[0:8], last, jnp.zeros((8, 8), F32)], axis=1)
    rall[window(rr), :] = rsend[0]
    fourth = start_all(3, [(rsend.at[0], rall.at[window(rr)], device) for r, device in column_to])
    if not backward:
        l1_copies = cross(1, l1buf.at[yy], lambda k: l1_source, blocks)
        start_cross(l1_copies)

    @pl.when(turn == yy)
    def _():
        l1buf[yy] = l1_source[...]

    finish(fourth)
    ninth = jnp.concatenate([rall[pl.ds(j, N_R, stride=8), :][:, 96:120] for j in range(4)], axis=1)
    f = jnp.concatenate([rall[:, 0:48], rall[:, 48:96], ninth[:, 0:48], ninth[:, 48:96]], axis=0)

    h = product(rows_ref, 2, f)
    for y in range(N_Y):
        pieces_of = [h[y * ROWS + 24 * x : y * ROWS + 24 * x + 24] for x in range(CX)]
        hsend[y] = pack(jnp.concatenate(pieces_of, axis=1), [total_local] if backward else [])
    hall[yy, gy] = hsend[yy]
    fifth = start_all(4, [(hsend.at[y], hall.at[yy, gy], device) for g, y, device in plane_to])

    finish_cross(1, l1buf, l1_source, owners)
    held = [l1buf[k] if backward else l1buf[k].reshape(C, 128) for k in range(4)]
    block = dot(jnp.concatenate(held, axis=1), gather_ref[...], NN, HIGHEST)
    if backward:
        gr, gi = block[:, 0:BLOCK], block[:, BLOCK : 2 * BLOCK]
        for i in range(C):
            mr, mi = modes_ref[i : i + 1, 0:BLOCK], modes_ref[i : i + 1, BLOCK : 2 * BLOCK]
            gs_ref[0, i] = mr * gr + mi * gi
            gs_ref[1, i] = mr * gi - mi * gr
    else:
        modes_out[...] = block
    finish(fifth)
    for y in range(N_Y):
        for g in range(N_GY):
            piece = hall[y, g]
            if backward:
                gl_ref[8 * g : 8 * g + 8, 8 * y : 8 * y + 8] = piece[24:32, 48:56] * FORWARD_SCALE
            for x, rows in enumerate(unpack(piece)):
                hall_out[x, g, :, y * 48 : y * 48 + 48] = rows
    for copy in started:
        copy.wait_send()
    for away, copy in l1_copies if backward else w_copies + l1_copies:
        pl.when(away)(copy.wait_send)


def pack(g, corner):
    tail = g[:, 128:144]
    width = 80 - 8 * len(corner)
    below = jnp.concatenate([tail[0:8], tail[8:16], tail[16:24], *corner, jnp.zeros((8, width), F32)], axis=1)
    return jnp.concatenate([g[:, 0:128], below], axis=0)


def unpack(message):
    below = message[24:32]
    tail = jnp.concatenate([below[:, 0:16], below[:, 16:32], below[:, 32:48]], axis=0)
    body = message[0:24]
    return [body[:, 0:48], body[:, 48:96], jnp.concatenate([body[:, 96:128], tail], axis=1)]


def product(rows_ref, first, values):
    high = values.astype(BF16)
    low = (values - high.astype(F32)).astype(BF16)
    both = dot(rows_ref[first], jnp.concatenate([high, low], axis=1), NN)
    width = values.shape[1]
    return both[:, :width] + both[:, width:] + dot(rows_ref[first + 1], high, NN)


def vmem():
    return pl.BlockSpec(memory_space=pltpu.VMEM)


def hbm():
    return pl.BlockSpec(memory_space=pltpu.HBM)


def comm_call(backward, field, tables, *operands):
    names = ["depth", "y", "rows", "expand", "keep", "gather"]
    outs = [jax.ShapeDtypeStruct((CX, N_GY, 24, 256), F32)]
    if backward:
        outs.append(jax.ShapeDtypeStruct((2, C, Q, BLOCK), F32))
        outs.append(jax.ShapeDtypeStruct((C, C), F32))
        kept = [vmem()] * 3
    else:
        outs.append(jax.ShapeDtypeStruct((C, 128), F32))
        outs.append(jax.ShapeDtypeStruct((2 * C * Q, 128), F32))
        kept = [hbm()] * 3
    pair = pltpu.SemaphoreType.DMA
    tile = (8, 128)
    scratch = [
        pltpu.VMEM((2 * K * Q, Q * TZ), BF16),
        pltpu.VMEM((2 * KY, 2 * Y), BF16),
        pltpu.VMEM((4, 288, 288), BF16),
        pltpu.VMEM((16, 128), F32),
        pltpu.VMEM((96, 128), F32),
        pltpu.VMEM((512, 128), F32),
        pltpu.VMEM((N_GY, CX, LANES, 256), BF16),
        pltpu.VMEM((N_GY, N_Y, 32, 128), F32),
        pltpu.VMEM((15, 32, 128), F32),
        pltpu.VMEM((288, 128), F32),
        pltpu.VMEM((128, 128), F32),
        pltpu.VMEM((15, *tile), F32),
        pltpu.VMEM((N_GY, *tile) if backward else (1, *tile), F32),
        pltpu.VMEM((N_GY - 1, *tile) if backward else (N_GY, *tile), F32),
        pltpu.VMEM((N_GY, 16, 128), F32),
        pltpu.VMEM((2, *tile), F32),
        pltpu.VMEM((128, 128), F32),
        pltpu.VMEM((N_Y, 32, 128), F32),
        pltpu.VMEM((N_Y, N_GY, 32, 128), F32),
        pltpu.VMEM((4, *tile) if backward else (4, N_GY, *tile), F32),
        pair((9,)),
        pair((2, 15)),
        pair((2, 15)),
        pair((2, 3)),
        pair((2, 15)),
        pair((2, 15)),
        pair((2, 4)),
        pair((2, 4)),
    ]
    if not backward:
        scratch += [
            pltpu.VMEM((2, C, Q, BLOCK), BF16),
            pltpu.VMEM((72, 128), F32),
            pltpu.VMEM((144, 128), F32),
            pltpu.VMEM((4, 8, 768), F32),
            pltpu.VMEM((4, 8, 768), F32),
            pltpu.VMEM((2, 8, 512), F32),
            pair((2,)),
            pltpu.VMEM((CX, C, TZ, Y), BF16),
            pair((CX,)),
        ]
    return pl.pallas_call(
        functools.partial(comm_kernel, backward),
        out_shape=outs,
        in_specs=[vmem() if backward else hbm()] + [hbm()] * len(names) + kept,
        out_specs=[vmem() for _ in outs],
        scratch_shapes=scratch,
        compiler_params=pltpu.CompilerParams(
            collective_id=1 if backward else 0,
            has_side_effects=True,
            vmem_limit_bytes=60 * 1024 * 1024,
        ),
        name="modes_backward" if backward else "modes_forward",
    )(field, *[tables[name] for name in names], *operands)


def spectral_rows(hall_ref, y_ref, depth_ref, gy, x, spec):
    for pair in range(2):
        halves = []
        for q in (2 * pair, 2 * pair + 1):
            h = hall_ref[x, q, :, 0:LANES]
            high = h.astype(BF16).astype(F32)
            stacked = jnp.concatenate([high, high, h - high], axis=0).astype(BF16)
            u = dot(stacked, y_ref[gy], TN)
            halves.append(jnp.concatenate([u[:, :Y], u[:, Y:]], axis=0).astype(BF16))
        s = dot(depth_ref[...], jnp.concatenate(halves, axis=1), NN)
        for h in range(2):
            q = 2 * pair + h
            spec[q * Q : (q + 1) * Q] = s[:, h * Y : (h + 1) * Y].reshape(Q, TZ, Y)


def chunk_of(ref, r):
    values = ref[:, r * 16 : (r + 1) * 16, :].astype(F32)
    return jnp.concatenate([values[:, 0:8].reshape(256, Y), values[:, 8:16].reshape(256, Y)], axis=1)


def unchunk(values):
    halves = [values[:, :Y].reshape(C, 8, Y), values[:, Y:].reshape(C, 8, Y)]
    return jnp.concatenate(halves, axis=1)


def channel_matrix(weight, repeat_ref, transposed):
    repeat = repeat_ref[...]
    half = dot(repeat, weight, NT_DIMS if transposed else NN).astype(BF16)
    full = dot(half, repeat, NT_DIMS)
    row = lax.broadcasted_iota(jnp.int32, full.shape, 0)
    col = lax.broadcasted_iota(jnp.int32, full.shape, 1)
    return jnp.where(row % 8 == col % 8, full, 0.0).astype(BF16)


def forward_kernel(field_ref, cot_ref, hall_ref, y_ref, depth_ref, lw_ref, repeat_ref, out_ref, grad_ref, local_ref, spec, acc, kron):
    x, gy = pl.program_id(0), lax.axis_index("gy")

    @pl.when(x == 0)
    def _():
        kron[...] = channel_matrix(lw_ref[...], repeat_ref, True)
        acc[...] = jnp.zeros_like(acc)

    spectral_rows(hall_ref, y_ref, depth_ref, gy, x, spec)
    for r in range(TZ // 16):
        cells = chunk_of(field_ref.at[:, 0], r).astype(BF16)
        pre = chunk_of(spec, r) + dot(kron[...], cells, NN)
        cdf = 0.5 * (1.0 + lax.erf(pre * ROOT_HALF))
        slope = cdf + pre * jnp.exp(-0.5 * pre * pre) * INV_ROOT_TWO_PI
        grad = chunk_of(cot_ref.at[:, 0], r) * slope
        out_ref[:, 0, r * 16 : (r + 1) * 16, :] = unchunk(pre * cdf).astype(BF16)
        grad_ref[:, 0, r * 16 : (r + 1) * 16, :] = unchunk(grad).astype(BF16)
        acc[...] += dot(cells, grad.astype(BF16), NT_DIMS)

    @pl.when(x == CX - 1)
    def _():
        row = lax.broadcasted_iota(jnp.int32, acc.shape, 0)
        col = lax.broadcasted_iota(jnp.int32, acc.shape, 1)
        kept = jnp.where(row % 8 == col % 8, acc[...], 0.0)
        repeat = repeat_ref[...].astype(F32)
        local_ref[...] = dot(dot(repeat, kept, TN, HIGHEST), repeat, NN, HIGHEST)


def backward_kernel(grad_ref, hall_ref, y_ref, depth_ref, lw_ref, repeat_ref, out_ref, spec, kron):
    x, gy = pl.program_id(0), lax.axis_index("gy")

    @pl.when(x == 0)
    def _():
        kron[...] = channel_matrix(lw_ref[...], repeat_ref, False)

    spectral_rows(hall_ref, y_ref, depth_ref, gy, x, spec)
    for r in range(TZ // 16):
        cells = chunk_of(grad_ref.at[:, 0], r).astype(BF16)
        total = chunk_of(spec, r) + dot(kron[...], cells, NN)
        out_ref[:, 0, r * 16 : (r + 1) * 16, :] = unchunk(total).astype(BF16)


def row_spec():
    return pl.BlockSpec((C, 1, TZ, Y), lambda x: (0, x, 0, 0))


def per_device(field_in, cotangent, spectral_weight, local_weight):
    cells = (C, CX, TZ, Y)
    field = field_in.reshape(cells)
    cot = cotangent.reshape(cells)
    weight = jnp.transpose(spectral_weight, (0, 2, 3, 1))
    depth = depth_table()
    tables = y_tables()
    high = tables.astype(BF16)
    low = (tables - high.astype(np.float64)).astype(BF16)
    depth_forward = jnp.asarray(depth.astype(BF16))
    depth_back = jnp.asarray(np.ascontiguousarray(depth.T).astype(BF16))
    y_forward = jnp.asarray(high)
    y_back = jnp.asarray(np.concatenate([high, low, high], axis=1))
    expand, keep = unit_tables()
    select, place, gather = owner_tables()
    forms = {
        "depth": depth_forward,
        "y": y_forward,
        "rows": jnp.asarray(row_tables()),
        "expand": jnp.asarray(expand),
        "keep": jnp.asarray(keep),
        "gather": jnp.asarray(gather.astype(np.float32)),
    }
    select, place = jnp.asarray(select.astype(np.float32)), jnp.asarray(place.astype(np.float32))
    repeat = jnp.asarray(np.repeat(np.eye(C), 8, axis=0).astype(BF16))

    hall, modes, owned = comm_call(False, field, forms, weight, select, place)
    field_shape = jax.ShapeDtypeStruct(cells, BF16)
    params = pltpu.CompilerParams(vmem_limit_bytes=60 * 1024 * 1024)
    output, grad_pre, local_terms = pl.pallas_call(
        forward_kernel,
        grid=(CX,),
        out_shape=[field_shape, field_shape, jax.ShapeDtypeStruct((C, C), F32)],
        in_specs=[row_spec(), row_spec()] + [vmem()] * 5,
        out_specs=[row_spec(), row_spec(), pl.BlockSpec((C, C), lambda x: (0, 0))],
        scratch_shapes=[pltpu.VMEM((C, TZ, Y), F32), pltpu.VMEM((256, 256), F32), pltpu.VMEM((256, 256), BF16)],
        compiler_params=params,
        name="cells_forward",
    )(field, cot, hall, y_back, depth_back, local_weight, repeat)
    hall, grad_spectral, grad_local = comm_call(True, grad_pre, forms, owned, modes, local_terms)
    grad_input = pl.pallas_call(
        backward_kernel,
        grid=(CX,),
        out_shape=field_shape,
        in_specs=[row_spec()] + [vmem()] * 5,
        out_specs=row_spec(),
        scratch_shapes=[pltpu.VMEM((C, TZ, Y), F32), pltpu.VMEM((256, 256), BF16)],
        compiler_params=params,
        name="cells_backward",
    )(grad_pre, hall, y_back, depth_back, local_weight, repeat)
    return (
        output.reshape(field_in.shape),
        grad_input.reshape(field_in.shape),
        jnp.transpose(grad_spectral, (0, 3, 1, 2)),
        grad_local,
    )


def solution(mesh):
    placed = (
        P(None, "slab", None, None, "gy"),
        P(None, "slab", None, None, "gy"),
        P(None, "slab", None, "gy"),
        P(),
    )
    return jax.shard_map(
        per_device,
        mesh=mesh,
        in_specs=placed,
        out_specs=(
            P(None, "slab", None, None, "gy"),
            P(None, "slab", None, None, "gy"),
            P(None, "slab", None, "gy"),
            P(),
        ),
        check_vma=False,
    )
```

time: 116 us -> 96.6 us (0.83)
  Pallas kernels: 106 us -> 94.3 us
  local copies, waits for them, and re-layouts: 6.93 us -> 1.32 us
  other arithmetic: 1.81 us -> 0 us
    pallas_call x2, Pallas kernels: 95.9 us -> 81 us  [comm_call(): pl.pallas_call(functools.partial(comm_kernel, backward), out_shape=outs,...]
    unnamed x26 -> x6, local copies, waits for them, and re-layouts: 6.93 us -> 1.32 us
    mul x1 -> x0, other arithmetic: 1.71 us -> none  [row_matrix(): return jnp.where(row % 12 == col % 12, value, 0.0) * FORWARD_SCALE]
    pallas_call x1, Pallas kernels: 3.84 us -> 5.43 us  [per_device(): pl.pallas_call(backward_kernel, grid=(CX,), out_shape=field_shape, in_spe...]
    pallas_call x1, Pallas kernels: 6.35 us -> 7.83 us  [per_device(): pl.pallas_call(forward_kernel, grid=(CX,), out_shape=[field_shape, field_...]
where the time goes in v2:
time: 96.6 us; the launch traced here: 96.3 us
  Pallas kernels  94.3 us (98%)
  local copies, waits for them, and re-layouts  1.32 us (1%)
    pallas_call x2, Pallas kernels, comm_call(): pl.pallas_call(functools.partial(comm_kernel, backward), out_shape=outs,...  81 us
    pallas_call x1, Pallas kernels, per_device(): pl.pallas_call(forward_kernel, grid=(CX,), out_shape=[field_shape, field_...  7.83 us
    pallas_call x1, Pallas kernels, per_device(): pl.pallas_call(backward_kernel, grid=(CX,), out_shape=field_shape, in_spe...  5.43 us

profile of v2, /device:TPU:1, one launch (start us, length us, event | category | flops | bytes accessed | tf_op | source)
XLA Modules:
  0.0 96.3 jit_solution(5103773969999026296)
XLA Ops:
  0.6 44.2 %modes_forward.1 = (f32[3,4,24,256]{3,2,1,0:T(8,128)}, f32[32,128]{1,0:T(8,128)}, f32[512,128]{1,0:T(8,128)}) custom-call(bf16[32,3,64,128]{3,2,1,0:T(8,128)(2,1)} %bitcast.6, bf16[384,512]{1,0:T(8,128)(2,1)} %constant.22.clone.refs_1_, bf16[4,24,256]{2,1,0:T(8,128)(2,1)} %constant.24.clone.refs_2_, bf16[16,4,288,288]{3,2,1,0:T(8,128)(2,1)} %constant.26.clone.refs_3_, ...), custom_call_target="tpu_custom_call" | custom-call | tf_op jit(solution)/shard_map/modes_forward/pallas_call | solution.py:532
  44.8 7.8 %cells_forward.1 = (bf16[32,3,64,128]{3,2,1,0:T(8,128)(2,1)}, bf16[32,3,64,128]{3,2,1,0:T(8,128)(2,1)}, f32[32,32]{1,0:T(8,128)}) custom-call(bf16[32,3,64,128]{3,2,1,0:T(8,128)(2,1)} %bitcast.7, bf16[32,3,64,128]{3,2,1,0:T(8,128)(2,1)} %bitcast.8, f32[3,4,24,256]{3,2,1,0:T(8,128)} %get-tuple-element.13.hall_ref, bf16[4,72,256]{2,1,0:T(8,128)(2,1)} %constant.25.clone.y_ref, ...), custom_call_target="tpu_custom_call" | custom-call | tf_op jit(solution)/shard_map/cells_forward/pallas_call | solution.py:656
  52.6 36.9 %modes_backward.1 = (f32[3,4,24,256]{3,2,1,0:T(8,128)}, f32[2,32,8,54]{3,2,1,0:T(8,128)}, f32[32,32]{1,0:T(8,128)}) custom-call(bf16[32,3,64,128]{3,2,1,0:T(8,128)(2,1)} %get-tuple-element.15.refs_0_.grad_ref, bf16[384,512]{1,0:T(8,128)(2,1)} %constant.22.clone.refs_1_, bf16[4,24,256]{2,1,0:T(8,128)(2,1)} %constant.24.clone.refs_2_, ...), custom_call_target="tpu_custom_call" | custom-call | tf_op jit(solution)/shard_map/modes_backward/pallas_call | solution.py:532
  89.5 0.0 copy-start
  89.5 0.0 copy-start.1
  89.5 5.4 %cells_backward.1 = bf16[32,3,64,128]{3,2,1,0:T(8,128)(2,1)} custom-call(bf16[32,3,64,128]{3,2,1,0:T(8,128)(2,1)} %get-tuple-element.15.refs_0_.grad_ref, f32[3,4,24,256]{3,2,1,0:T(8,128)} %get-tuple-element.19.hall_ref, bf16[4,72,256]{2,1,0:T(8,128)(2,1)} %constant.25.clone.y_ref, bf16[512,384]{1,0:T(8,128)(2,1)} %constant.23.clone.depth_ref, ...), custom_call_target="tpu_custom_call" | custom-call | tf_op jit(solution)/shard_map/cells_backward/pallas_call | solution.py:667
  95.0 0.0 copy-done
  95.0 0.7 copy.21
  95.7 0.0 copy-done.1
  95.7 0.6 copy.22
Async XLA Ops:
  89.5 5.5 %copy-start = (f32[2,32,8,54]{3,2,1,0:T(8,128)S(1)}, f32[2,32,8,54]{3,2,1,0:T(8,128)}, u32[]{:S(2)}) copy-start(f32[2,32,8,54]{3,2,1,0:T(8,128)} %get-tuple-element.20) | copy-start | bytes 331780
  89.5 6.2 %copy-start.1 = (f32[32,32]{1,0:T(8,128)S(1)}, f32[32,32]{1,0:T(8,128)}, u32[]{:S(2)}) copy-start(f32[32,32]{1,0:T(8,128)} %get-tuple-element.29) | copy-start | bytes 12292

commit v3 on v0

v3 whole, which is shorter than its diff:
```python
import functools
import math
import types

import jax
import jax.numpy as jnp
import numpy as np
from jax import lax
from jax.experimental import pallas as pl
from jax.experimental.pallas import tpu as pltpu
from jax.sharding import PartitionSpec as P

C = 32
KX = 12
KY = 12
KZ = 12
NT = 2
NZ = 32
NX = 192
NY = 512
CX = 3
N_GY = 4
N_Y = 4
N_R = 16
Q = C // N_GY
K = NT * KZ
TZ = NT * NZ
Y = NY // N_GY
BLOCK = 54
OWN = 27
UNITS = 9
ROWS = 72
LANES = K * Q

FORWARD_SCALE = 1.0 / math.sqrt(NX * NY * NZ * NT)
INVERSE_SCALE = 1.0 / math.sqrt(KX * KY * KZ * NT)
ROOT_HALF = 0.7071067811865476
INV_ROOT_TWO_PI = 0.3989422804014327
HIGHEST = lax.Precision.HIGHEST
WINDOW = [(z % 4) * 4 + x * 2 + z // 4 for x in range(2) for z in range(8)]
PLANE = [(h, c, y) for h in range(2) for c in range(2) for y in range(N_Y) if (h, c, y) != (0, 0, 0)]
PLANE.sort(key=lambda d: -(2 * d[0] + min(d[2], N_Y - d[2])))
COLUMN = [(x, z) for x in range(2) for z in range(8) if (x, z) != (0, 0)]
COLUMN.sort(key=lambda d: -(d[0] + min(d[1], 8 - d[1])))
F32 = jnp.float32
BF16 = jnp.bfloat16
MESH = pl.DeviceIdType.MESH


def frequencies(kept):
    values = np.arange(kept)
    return np.where(values < kept // 2, values, values - kept)


def depth_table():
    t, z = np.divmod(np.arange(TZ), NZ)
    kt, kz = np.divmod(np.arange(K), KZ)
    product = (t[None] * kt[:, None] * NZ + z[None] * frequencies(KZ)[kz][:, None] * NT) % TZ
    angle = product * (2.0 * np.pi / TZ)
    parts = np.stack([np.cos(angle), -np.sin(angle)])
    full = np.einsum("pks,cd->pkcds", parts, np.eye(Q))
    return full.reshape(2 * K * Q, Q * TZ)


def y_tables():
    product = (frequencies(KY)[:, None] * np.arange(NY)[None]) % NY
    angle = product * (2.0 * np.pi / NY)
    cos, sin = np.cos(angle), np.sin(angle)
    full = np.stack([np.stack([cos, sin]), np.stack([-sin, cos])])
    full = full.reshape(2, 2, KY, N_GY, Y).transpose(3, 0, 2, 1, 4)
    return full.reshape(N_GY, 2 * KY, 2 * Y)


def unit_tables():
    lane = np.arange(128)
    row = np.arange(96)
    expand = (lane[None] // 3 == np.arange(16)[:, None]) & (lane[None] < OWN)
    keep = ((row[:, None] // 8) % 3 == lane[None] % 3) & (lane[None] < OWN)
    return expand.astype(np.float32), keep.astype(np.float32)


def row_tables():
    main = [9 * w + j for w in WINDOW for j in range(8)]
    ninth = [9 * w + 8 for w in WINDOW]
    pairs = np.array(main + main + ninth + ninth)
    part = np.array([0] * 128 + [1] * 128 + [0] * 16 + [1] * 16)
    y, x, part_in, ky = np.unravel_index(np.arange(288), (N_Y, CX, 2, KY))
    row = 48 * y[None] + 3 * np.arange(N_R)[:, None] + x[None]
    freq = frequencies(KX)[pairs // KY]
    angle = (freq[None, :, None] * row[:, None, :]) % NX * (2.0 * np.pi / NX)
    sign = np.where(part == 0, 1.0, -1.0)[:, None]
    value = np.where(part[:, None] == part_in[None], np.cos(angle), sign * np.sin(angle))
    value = np.where((pairs % KY)[:, None] == ky[None], value, 0.0)
    forward, inverse = value * FORWARD_SCALE, value.transpose(0, 2, 1) * INVERSE_SCALE
    parts = []
    for full in (forward, inverse):
        high = full.astype(BF16)
        parts += [high, (full - high.astype(np.float64)).astype(BF16)]
    return np.stack(parts, axis=1)


def owner_tables():
    select = np.zeros((4, 72, 128))
    place = np.zeros((8, 72, 128))
    gather = np.zeros((4, 8, OWN, 128))
    for t in range(4):
        count = [0] * 8
        for mode in range(BLOCK):
            unit = 18 * t + mode // 3
            part, other = unit % 8, 3 * (unit // 8) + mode % 3
            n = count[part]
            count[part] += 1
            select[t, 8 * part + n if n < 8 else 64 + part - 2 * t, mode] = 1.0
            for x in range(2):
                place[part, 16 * t + 8 * x + n if n < 8 else 64 + x, OWN * x + other] = 1.0
            gather[t, part, other, mode] = 1.0
    return select, place, gather.reshape(4, 8 * OWN, 128)


def dot(a, b, dims, precision=None):
    return lax.dot_general(a, b, (dims, ((), ())), precision=precision, preferred_element_type=F32)


NN = ((1,), (0,))
NT_DIMS = ((1,), (1,))
TN = ((0,), (0,))


def pack(g, corner):
    tail = g[:, 128:144]
    width = 80 - 8 * len(corner)
    below = jnp.concatenate([tail[0:8], tail[8:16], tail[16:24], *corner, jnp.zeros((8, width), F32)], axis=1)
    return jnp.concatenate([g[:, 0:128], below], axis=0)


def unpack(message):
    below = message[24:32]
    tail = jnp.concatenate([below[:, 0:16], below[:, 16:32], below[:, 32:48]], axis=0)
    body = message[0:24]
    return [body[:, 0:48], body[:, 48:96], jnp.concatenate([body[:, 96:128], tail], axis=1)]


def product(rows_ref, first, values):
    high = values.astype(BF16)
    low = (values - high.astype(F32)).astype(BF16)
    both = dot(rows_ref[first], jnp.concatenate([high, low], axis=1), NN)
    width = values.shape[1]
    return both[:, :width] + both[:, width:] + dot(rows_ref[first + 1], high, NN)


def chunk_of(values):
    values = values.astype(F32)
    return jnp.concatenate([values[:, 0:8].reshape(256, Y), values[:, 8:16].reshape(256, Y)], axis=1)


def unchunk(values):
    halves = [values[:, :Y].reshape(C, 8, Y), values[:, Y:].reshape(C, 8, Y)]
    return jnp.concatenate(halves, axis=1)


def same_row(shape):
    row = lax.broadcasted_iota(jnp.int32, shape, 0)
    col = lax.broadcasted_iota(jnp.int32, shape, 1)
    return row % 8 == col % 8


def channel_matrix(weight, repeat, transposed):
    half = dot(repeat, weight, NT_DIMS if transposed else NN).astype(BF16)
    full = dot(half, repeat, NT_DIMS)
    return jnp.where(same_row(full.shape), full, 0.0).astype(BF16)


CHUNKS = TZ // 16
BIG = (32, 128)
TILE = (8, 128)
DMA = pltpu.SemaphoreType.DMA

INPUTS = ["field", "cot", "weight", "lw", "depth", "depth_back", "y_table", "y_back", "rows", "expand", "keep"]
INPUTS += ["select", "place", "gather", "repeat"]
OUTPUTS = ["out", "grad_in", "grad_spectral", "grad_local"]
SCRATCH = {
    "v_field": ((CX, C, TZ, Y), BF16),
    "v_cot": ((CX, C, TZ, Y), BF16),
    "v_weight": ((2, C, Q, BLOCK), BF16),
    "v_lw": ((C, C), BF16),
    "v_depth": ((2 * K * Q, Q * TZ), BF16),
    "v_depth_back": ((Q * TZ, 2 * K * Q), BF16),
    "v_y_table": ((2 * KY, 2 * Y), BF16),
    "v_y_back": ((6 * KY, 2 * Y), BF16),
    "v_rows": ((4, 288, 288), BF16),
    "v_expand": ((16, 128), F32),
    "v_keep": ((96, 128), F32),
    "v_select": ((72, 128), F32),
    "v_place": ((72, 128), F32),
    "v_gather": ((8 * OWN, 128), F32),
    "v_repeat": ((256, C), BF16),
    "grad_pre": ((CX, C, TZ, Y), BF16),
    "spec": ((C, TZ, Y), F32),
    "cells": ((CX * CHUNKS, 256, 256), BF16),
    "cot_cells": ((CX * CHUNKS, 256, 256), F32),
    "local_part": ((CX * CHUNKS, 256, 256), F32),
    "acc": ((256, 256), F32),
    "z_all": ((N_GY, CX, LANES, 256), F32),
    "gsend": ((2, N_GY, N_Y, *BIG), F32),
    "grecv": ((2, 15, *BIG), F32),
    "g12": ((288, 128), F32),
    "msend": ((2, 128, 128), F32),
    "mrecv": ((2, 15, *TILE), F32),
    "qbuf": ((2, *TILE), F32),
    "qsend": ((2, *TILE), F32),
    "qrecv": (TILE, F32),
    "sums": ((N_GY, 16, 128), F32),
    "grads": (TILE, F32),
    "rsend": ((2, *TILE), F32),
    "rall": ((2, 128, 128), F32),
    "hsend": ((2, N_Y, *BIG), F32),
    "hall": ((2, N_Y, N_GY, *BIG), F32),
    "hx": ((CX, N_GY, 24, 256), F32),
    "wsend": ((8, 8, 512), F32),
    "wrecv": ((8, 8, 512), F32),
    "esend": ((2, *TILE), F32),
    "erecv": ((2, *TILE), F32),
    "owned": ((2 * C * Q, 128), F32),
    "home_modes": ((8, 2, *TILE), F32),
    "home_grads": ((8, *TILE), F32),
    "block_modes": ((64, 128), F32),
}
SEMAPHORES = {
    "load_sem": (13,),
    "cell_sem": (2, CX),
    "plane_sem": (2, 2, 2, 15),
    "column_sem": (2, 2, 2, 15),
    "core_sem": (2, 2),
    "w_sem": (2, 8),
    "e_sem": (2, 2),
    "home_sem": (2, 2, 8),
}


def layer_kernel(*refs):
    ref = types.SimpleNamespace(**dict(zip(INPUTS + OUTPUTS + list(SCRATCH) + list(SEMAPHORES), refs)))

    slab, gy = lax.axis_index("slab"), lax.axis_index("gy")
    yy, rr = lax.div(slab, N_R), lax.rem(slab, N_R)
    x_hi, core = lax.div(gy, 2), lax.rem(gy, 2)
    x_lo, z = lax.div(rr, 8), lax.rem(rr, 8)
    turn, half = lax.rem(z, 4), lax.div(z, 4)
    mine = 4 * x_hi + yy
    near = x_lo * 8 + half * 4

    sources = {
        "depth": ref.depth,
        "y_table": ref.y_table.at[gy],
        "weight": ref.weight,
        "select": ref.select.at[turn],
        "place": ref.place.at[mine],
        "rows": ref.rows.at[rr],
        "expand": ref.expand,
        "keep": ref.keep,
        "gather": ref.gather.at[turn],
        "lw": ref.lw,
        "repeat": ref.repeat,
        "depth_back": ref.depth_back,
        "y_back": ref.y_back.at[gy],
    }
    loads = {
        name: pltpu.make_async_copy(source, getattr(ref, "v_" + name), ref.load_sem.at[k])
        for k, (name, source) in enumerate(sources.items())
    }
    fields = [pltpu.make_async_copy(ref.field.at[:, x], ref.v_field.at[x], ref.cell_sem.at[0, x]) for x in range(CX)]
    cots = [pltpu.make_async_copy(ref.cot.at[:, x], ref.v_cot.at[x], ref.cell_sem.at[1, x]) for x in range(CX)]
    fields[0].start()
    loads["depth"].start()
    loads["y_table"].start()
    fields[1].start()
    fields[2].start()
    for name in list(loads)[2:]:
        loads[name].start()
    for copy in cots:
        copy.start()

    def ready(*names):
        for name in names:
            loads[name].wait()

    def plane(k):
        d_hi, d_core, dy = PLANE[k]
        g_to = lax.rem(x_hi + d_hi, 2) * 2 + lax.rem(core + d_core, 2)
        y_to = lax.rem(yy + dy, N_Y)
        return g_to, y_to, {"gy": g_to, "slab": y_to * N_R + rr}

    def column(k):
        d_lo, dz = COLUMN[k]
        r_to = lax.rem(x_lo + d_lo, 2) * 8 + lax.rem(z + dz, 8)
        return r_to, {"slab": yy * N_R + r_to}

    def across(slab_of):
        found = []
        for d_hi in range(2):
            to_hi = lax.rem(x_hi + d_hi, 2)
            for k in range(4):
                to = slab_of(k)
                found.append((to_hi, k, to, (to != slab) if d_hi == 0 else None))
        return found

    owners = across(lambda k: k * N_R + near + yy)
    blocks = across(lambda k: turn * N_R + near + k)
    at_home = (turn == yy).astype(jnp.int32)

    def guarded(away, action):
        if away is None:
            action()
        else:
            pl.when(away)(action)

    def device_of(to_hi, to):
        return {"gy": to_hi * 2 + core, "slab": to}

    barrier = pltpu.get_barrier_semaphore()

    def greet(device):
        pl.semaphore_signal(barrier, inc=1, device_id=device, device_id_type=MESH)

    for k in range(15):
        greet(plane(k)[2])
        greet(column(k)[1])
    for to_hi, _, to, away in owners + blocks:
        guarded(away, functools.partial(greet, device_of(to_hi, to)))

    def copy_to(source, target, send_sem, recv_sem, device):
        return pltpu.make_async_remote_copy(
            src_ref=source,
            dst_ref=target,
            send_sem=send_sem,
            recv_sem=recv_sem,
            device_id=device,
            device_id_type=MESH,
        )

    started = []

    def start_all(sem, copies):
        made = [copy_to(a, b, sem.at[0, k], sem.at[1, k], device) for k, (a, b, device) in enumerate(copies)]
        for copy in made:
            copy.start()
        started.extend((None, copy) for copy in made)
        return made

    def finish(made):
        for copy in made:
            copy.wait_recv()

    plane_to = [plane(k) for k in range(15)]
    column_to = [column(k) for k in range(15)]
    slot = {d: k for k, d in enumerate(PLANE)}

    def window(r):
        return pl.ds(pl.multiple_of(r * 8, 8), 8)

    def send_home(index, source, target):
        sem = ref.home_sem.at[index]
        for k, (to_hi, _, to, away) in enumerate(blocks):
            copy = copy_to(source, target.at[mine], sem.at[0, k], sem.at[1, mine], device_of(to_hi, to))
            guarded(away, copy.start)
            started.append((away, copy))

        @pl.when(turn == yy)
        def _():
            target[mine] = source[...]

    def come_home(index, source, target):
        sem = ref.home_sem.at[index]
        for k, (from_hi, y, origin, away) in enumerate(owners):
            place = 4 * from_hi + y
            copy = copy_to(source, target.at[place], sem.at[0, k], sem.at[1, place], device_of(from_hi, origin))
            guarded(away, copy.wait_recv)

    def in_block_order(messages):
        rows = []
        for n in range(4):
            rows.append(jnp.concatenate([m[:, OWN * n : OWN * n + OWN] for m in messages], axis=1))
        return dot(jnp.concatenate(rows, axis=0), ref.v_gather[...], NN, HIGHEST)

    def depth_stage(cells_of, x):
        for pair in range(2):
            pieces = [cells_of(x, slice((2 * pair + h) * Q, (2 * pair + h + 1) * Q)).reshape(Q * TZ, Y) for h in range(2)]
            zz = dot(ref.v_depth[...], jnp.concatenate(pieces, axis=1), NN)
            for h in range(2):
                part = zz[:, h * Y : (h + 1) * Y]
                ref.z_all[2 * pair + h, x, :, 0:Y] = part[:LANES]
                ref.z_all[2 * pair + h, x, :, Y:] = part[LANES:]

    def to_window(index, local, beside_first, beside_second):
        table = ref.v_y_table[...]
        gsend, grecv = ref.gsend.at[index], ref.grecv.at[index]
        for g in range(N_GY):
            for y in range(N_Y):
                lanes = slice(24 * (4 * (g // 2) + y), 24 * (4 * (g // 2) + y) + 24)
                rows = [ref.z_all[q, x, lanes, :] for x in range(CX) for q in (g % 2, g % 2 + 2)]
                piece = dot(table, jnp.concatenate(rows, axis=0).astype(BF16), NT_DIMS)
                corner = [] if local is None else [local[8 * g : 8 * g + 8, 8 * y : 8 * y + 8]]
                gsend[g, y] = pack(piece, corner)
        if index == 0:
            pl.semaphore_wait(barrier, 30 + 16 - 2 * at_home)
        sem = ref.plane_sem.at[index, 0]
        first = start_all(sem, [(gsend.at[g, y], grecv.at[k], to) for k, (g, y, to) in enumerate(plane_to)])
        beside_first()
        finish(first)
        block = jnp.zeros((8, 8), F32)
        for dy in range(N_Y):
            total = gsend[gy, yy] if dy == 0 else None
            for d_hi in range(2):
                for d_core in range(2):
                    if (d_hi, d_core, dy) in slot:
                        term = grecv[slot[d_hi, d_core, dy]]
                        total = term if total is None else total + term
            block = block + total[24:32, 48:56]
            base = lax.rem(yy + N_Y - dy, N_Y) * ROWS
            for x, piece in enumerate(unpack(total)):
                ref.g12[pl.ds(pl.multiple_of(base + 24 * x, 8), 24), 0:48] = piece

        f = product(ref.v_rows, 0, ref.g12[:, 0:48])
        msend, mrecv = ref.msend.at[index], ref.mrecv.at[index]
        blank = jnp.zeros((128, 24), F32)
        msend[...] = jnp.concatenate([f[0:128], f[128:256], blank, jnp.concatenate([block] * N_R, axis=0)], axis=1)
        ninth = jnp.concatenate([f[256:272], f[272:288]], axis=1)
        for j in range(4):
            old = msend[pl.ds(j, N_R, stride=8), :]
            msend[pl.ds(j, N_R, stride=8), :] = jnp.concatenate(
                [old[:, 0:96], ninth[:, 24 * j : 24 * j + 24], old[:, 120:128]], axis=1
            )
        sem = ref.column_sem.at[index, 0]
        second = start_all(sem, [(msend.at[window(r)], mrecv.at[k], to) for k, (r, to) in enumerate(column_to)])
        beside_second()
        finish(second)
        m = msend[window(rr), :]
        for k in range(15):
            m = m + mrecv[k]

        last = jnp.concatenate([m[j : j + 1, 96:120] for j in range(4)], axis=1)
        nine = jnp.concatenate([m[:, 0:96], last, jnp.zeros((7, 96), F32)], axis=0)
        spread = dot(nine, ref.v_expand[...], TN, HIGHEST) * ref.v_keep[...]
        parts = {}
        for n in range(4):
            base = 24 * n
            total = spread[base : base + 8] + spread[base + 8 : base + 16] + spread[base + 16 : base + 24]
            parts[n // 2, n % 2] = total[:, 0:OWN]
        return parts, m[:, 120:128]

    def packed(parts):
        end = jnp.zeros((Q, 128 - 4 * OWN), F32)
        return jnp.concatenate([parts[part, h] for h in range(2) for part in range(2)] + [end], axis=1)

    def from_mixed(index, mixed, corner, beside_first, beside_second):
        pad = jnp.zeros((Q, 128 - OWN), F32)
        wide = [jnp.concatenate([mixed[part, h], pad], axis=1) for part in range(2) for h in range(2)]
        tiled = jnp.concatenate([v for v in wide for _ in range(3)], axis=0) * ref.v_keep[...]
        u = dot(ref.v_expand[...], tiled, NT_DIMS, HIGHEST)
        last = jnp.concatenate([u[8:9, 24 * j : 24 * j + 24] for j in range(4)] + [jnp.zeros((4, 24), F32)], axis=0)
        rsend, rall = ref.rsend.at[index], ref.rall.at[index]
        rsend[...] = jnp.concatenate([u[0:8], last, jnp.zeros((8, 8), F32)], axis=1)
        rall[window(rr), :] = rsend[...]
        sem = ref.column_sem.at[index, 1]
        third = start_all(sem, [(rsend, rall.at[window(rr)], to) for _, to in column_to])
        beside_first()
        finish(third)
        ninth = jnp.concatenate([rall[pl.ds(j, N_R, stride=8), :][:, 96:120] for j in range(4)], axis=1)
        f = jnp.concatenate([rall[:, 0:48], rall[:, 48:96], ninth[:, 0:48], ninth[:, 48:96]], axis=0)
        h = product(ref.v_rows, 2, f)
        hsend, hall = ref.hsend.at[index], ref.hall.at[index]
        for y in range(N_Y):
            rows = [h[y * ROWS + 24 * x : y * ROWS + 24 * x + 24] for x in range(CX)]
            hsend[y] = pack(jnp.concatenate(rows, axis=1), corner)
        hall[yy, gy] = hsend[yy]
        sem = ref.plane_sem.at[index, 1]
        fourth = start_all(sem, [(hsend.at[y], hall.at[yy, gy], to) for _, y, to in plane_to])
        beside_second()
        finish(fourth)
        for y in range(N_Y):
            for g in range(N_GY):
                base = 24 * (4 * (g // 2) + y)
                for x, piece in enumerate(unpack(hall[y, g])):
                    for h in range(2):
                        ref.hx[x, 2 * h + g % 2, :, base : base + 24] = piece[:, 24 * h : 24 * h + 24]

    def spectral_rows(x):
        for pair in range(2):
            halves = []
            for q in (2 * pair, 2 * pair + 1):
                h = ref.hx[x, q, :, 0:LANES]
                high = h.astype(BF16).astype(F32)
                stacked = jnp.concatenate([high, high, h - high], axis=0).astype(BF16)
                u = dot(stacked, ref.v_y_back[...], TN)
                halves.append(jnp.concatenate([u[:, :Y], u[:, Y:]], axis=0).astype(BF16))
            s = dot(ref.v_depth_back[...], jnp.concatenate(halves, axis=1), NN)
            for h in range(2):
                q = 2 * pair + h
                ref.spec[q * Q : (q + 1) * Q] = s[:, h * Y : (h + 1) * Y].reshape(Q, TZ, Y)

    ready("depth", "y_table")
    for x in range(CX):
        fields[x].wait()
        depth_stage(lambda x, c: ref.v_field[x, c], x)

    def send_weights():
        ready("weight", "select", "place")
        flat = ref.v_weight[...].astype(F32).reshape(2 * C * Q, BLOCK).astype(BF16)
        picked = dot(ref.v_select[...][:, 0:BLOCK].astype(BF16), flat, NT_DIMS)
        for k in range(8):
            ref.wsend[k] = picked[8 * k : 8 * k + 8]
        for e in range(2):
            row = picked[64 + e : 65 + e]
            lanes = [row[:, 128 * j : 128 * j + 128] for j in range(4)]
            ref.esend[e] = jnp.concatenate([*lanes, jnp.zeros((4, 128), F32)], axis=0)
        own = 2 * turn + x_hi
        for k, (to_hi, y, to, away) in enumerate(owners):
            source = ref.wsend.at[4 * to_hi + y]
            copy = copy_to(source, ref.wrecv.at[own], ref.w_sem.at[0, k], ref.w_sem.at[1, own], device_of(to_hi, to))
            guarded(away, copy.start)
            started.append((away, copy))
        for e in range(2):
            to_hi, y = lax.div(turn, 2), lax.rem(2 * turn, 4) + e
            to = y * N_R + near + yy
            copy = copy_to(
                ref.esend.at[e], ref.erecv.at[x_hi], ref.e_sem.at[0, e], ref.e_sem.at[1, x_hi], device_of(to_hi, to)
            )
            here = jnp.logical_and(to_hi == x_hi, to == slab)
            away = jnp.logical_not(here)
            pl.when(away)(copy.start)
            started.append((away, copy))

            @pl.when(here)
            def _():
                ref.erecv[x_hi] = ref.esend[e]

        @pl.when(turn == yy)
        def _():
            ref.wrecv[own] = ref.wsend[mine]

        ready("rows", "expand", "keep")

    def receive_weights():
        for k, (from_hi, t, origin, away) in enumerate(blocks):
            at = 2 * t + from_hi
            copy = copy_to(
                ref.wsend.at[0], ref.wrecv.at[at], ref.w_sem.at[0, k], ref.w_sem.at[1, at], device_of(from_hi, origin)
            )
            guarded(away, copy.wait_recv)
        origin = turn * N_R + near + lax.div(mine, 2)
        for hi in range(2):
            copy = copy_to(
                ref.esend.at[0], ref.erecv.at[hi], ref.e_sem.at[0, hi], ref.e_sem.at[1, hi], device_of(hi, origin)
            )
            pl.when(jnp.logical_or(x_hi != hi, origin != slab))(copy.wait_recv)
        ninths = [jnp.concatenate([ref.erecv[hi, j : j + 1, :] for j in range(4)], axis=1) for hi in range(2)]
        received = jnp.concatenate([ref.wrecv[...].reshape(64, 512), *ninths, jnp.zeros((6, 512), F32)], axis=0)
        ref.owned[...] = dot(received.astype(BF16), ref.v_place[...].astype(BF16), TN)

    def local_products(weight_transposed, cells_of):
        kron = channel_matrix(ref.v_lw[...], ref.v_repeat[...], weight_transposed)
        for n in range(CX * CHUNKS):
            ref.local_part[n] = dot(kron, cells_of(n), NN)

    def prepare_cells():
        ready("lw", "repeat", "depth_back", "y_back", "gather")
        for copy in cots:
            copy.wait()
        for x in range(CX):
            for r in range(CHUNKS):
                n = x * CHUNKS + r
                ref.cells[n] = chunk_of(ref.v_field[x, :, 16 * r : 16 * r + 16, :]).astype(BF16)
                ref.cot_cells[n] = chunk_of(ref.v_cot[x, :, 16 * r : 16 * r + 16, :])

    def beside_column():
        receive_weights()
        prepare_cells()

    parts, _ = to_window(0, None, send_weights, beside_column)

    other_core = {"gy": x_hi * 2 + 1 - core}
    ref.qbuf[core] = packed(parts)
    copy = copy_to(ref.qbuf.at[core], ref.qbuf.at[core], ref.core_sem.at[0, 0], ref.core_sem.at[0, 1], other_core)
    copy.start()
    copy.wait_recv()
    started.append((None, copy))
    mixed_r = jnp.zeros((Q, BLOCK), F32)
    mixed_i = jnp.zeros((Q, BLOCK), F32)

    def weights(i):
        return ref.owned[8 * i : 8 * i + 8, 0:BLOCK], ref.owned[256 + 8 * i : 264 + 8 * i, 0:BLOCK]

    for q in range(N_GY):
        both = ref.qbuf[q % 2]
        base = 2 * OWN * (q // 2)
        real, imag = both[:, base : base + OWN], both[:, base + OWN : base + 2 * OWN]
        real, imag = jnp.concatenate([real, real], axis=1), jnp.concatenate([imag, imag], axis=1)
        for c in range(Q):
            mr, mi = real[c : c + 1], imag[c : c + 1]
            w0, w1 = weights(q * Q + c)
            mixed_r = mixed_r + (mr * w0 - mi * w1)
            mixed_i = mixed_i + (mr * w1 + mi * w0)
    mixed = {(p, h): v[:, OWN * h : OWN * h + OWN] for p, v in enumerate((mixed_r, mixed_i)) for h in range(2)}

    def beside_modes():
        send_home(0, ref.qbuf, ref.home_modes)
        local_products(True, lambda n: ref.cells[n])

    def modes_home():
        come_home(0, ref.qbuf, ref.home_modes)
        ref.block_modes[...] = in_block_order([ref.home_modes[k].reshape(16, 128) for k in range(8)])

    from_mixed(0, mixed, [], beside_modes, modes_home)

    ref.acc[...] = jnp.zeros_like(ref.acc)
    for x in range(CX):
        spectral_rows(x)
        for r in range(CHUNKS):
            n = x * CHUNKS + r
            rows = slice(16 * r, 16 * r + 16)
            pre = chunk_of(ref.spec[:, rows, :]) + ref.local_part[n]
            cdf = 0.5 * (1.0 + lax.erf(pre * ROOT_HALF))
            slope = cdf + pre * jnp.exp(-0.5 * pre * pre) * INV_ROOT_TWO_PI
            grad = ref.cot_cells[n] * slope
            ref.out[:, x, rows, :] = unchunk(pre * cdf).astype(BF16)
            ref.grad_pre[x, :, rows, :] = unchunk(grad).astype(BF16)
            ref.acc[...] += dot(ref.cells[n], grad.astype(BF16), NT_DIMS)
        depth_stage(lambda x, c: ref.grad_pre[x, c], x)
    kept = jnp.where(same_row((256, 256)), ref.acc[...], 0.0)
    repeat = ref.v_repeat[...].astype(F32)
    local = dot(dot(repeat, kept, TN, HIGHEST), repeat, NN, HIGHEST)

    def chunk_grad(n):
        x, r = divmod(n, CHUNKS)
        return chunk_of(ref.grad_pre[x, :, 16 * r : 16 * r + 16, :]).astype(BF16)

    parts, total_local = to_window(1, local, lambda: None, lambda: local_products(False, chunk_grad))
    ref.grads[...] = packed(parts)
    gr, gi = (jnp.concatenate([parts[p, 0], parts[p, 1]], axis=1) for p in range(2))
    for i in range(C):
        q, c = divmod(i, Q)
        w0, w1 = weights(i)
        ref.sums[q, c : c + 1, 0:BLOCK] = jnp.sum(gr * w0 + gi * w1, axis=0, keepdims=True)
        ref.sums[q, 8 + c : 9 + c, 0:BLOCK] = jnp.sum(gi * w0 - gr * w1, axis=0, keepdims=True)
    for k in range(2):
        found = {}
        for h in range(2):
            both = ref.sums[2 * h + k]
            both = both[:, 0:OWN] + both[:, OWN:BLOCK]
            found[0, h], found[1, h] = both[0:8], both[8:16]
        ref.qsend[k] = packed(found)
    copy = copy_to(ref.qsend.at[1 - core], ref.qrecv, ref.core_sem.at[1, 0], ref.core_sem.at[1, 1], other_core)
    copy.start()
    copy.wait_recv()
    started.append((None, copy))
    both = ref.qsend[core] + ref.qrecv[...]
    mixed = {(p, h): both[:, OWN * (2 * h + p) : OWN * (2 * h + p) + OWN] for p in range(2) for h in range(2)}

    def weight_gradient():
        come_home(1, ref.grads, ref.home_grads)
        grads = in_block_order([ref.home_grads[k] for k in range(8)])
        grads = jnp.where(x_hi == 0, grads[0:16], grads[16:32])
        gr, gi = grads[0:8, 0:BLOCK], grads[8:16, 0:BLOCK]
        for i in range(C):
            q, c = divmod(i, Q)
            row = 32 * (q // 2) + 8 * (q % 2) + c
            mr, mi = ref.block_modes[row : row + 1, 0:BLOCK], ref.block_modes[row + 16 : row + 17, 0:BLOCK]
            ref.grad_spectral[0, i] = mr * gr + mi * gi
            ref.grad_spectral[1, i] = mr * gi - mi * gr

    from_mixed(1, mixed, [total_local], lambda: send_home(1, ref.grads, ref.home_grads), weight_gradient)
    for y in range(N_Y):
        for g in range(N_GY):
            corner = ref.hall[1, y, g, 24:32, 48:56]
            ref.grad_local[8 * g : 8 * g + 8, 8 * y : 8 * y + 8] = corner * FORWARD_SCALE
    for x in range(CX):
        spectral_rows(x)
        for r in range(CHUNKS):
            rows = slice(16 * r, 16 * r + 16)
            total = chunk_of(ref.spec[:, rows, :]) + ref.local_part[x * CHUNKS + r]
            ref.grad_in[:, x, rows, :] = unchunk(total).astype(BF16)
    for away, copy in started:
        guarded(away, copy.wait_send)


def per_device(field_in, cotangent, spectral_weight, local_weight):
    cells = (C, CX, TZ, Y)
    depth = depth_table()
    tables = y_tables()
    high = tables.astype(BF16)
    low = (tables - high.astype(np.float64)).astype(BF16)
    expand, keep = unit_tables()
    select, place, gather = owner_tables()
    values = {
        "field": field_in.reshape(cells),
        "cot": cotangent.reshape(cells),
        "weight": jnp.transpose(spectral_weight, (0, 2, 3, 1)),
        "lw": local_weight,
        "depth": depth.astype(BF16),
        "depth_back": np.ascontiguousarray(depth.T).astype(BF16),
        "y_table": high,
        "y_back": np.concatenate([high, low, high], axis=1),
        "rows": row_tables(),
        "expand": expand,
        "keep": keep,
        "select": select.astype(np.float32),
        "place": place.astype(np.float32),
        "gather": gather.astype(np.float32),
        "repeat": np.repeat(np.eye(C), 8, axis=0).astype(BF16),
    }
    outs = [(cells, BF16), (cells, BF16), ((2, C, Q, BLOCK), F32), ((C, C), F32)]
    output, grad_input, grad_spectral, grad_local = pl.pallas_call(
        layer_kernel,
        out_shape=[jax.ShapeDtypeStruct(shape, dtype) for shape, dtype in outs],
        in_specs=[pl.BlockSpec(memory_space=pltpu.HBM) for _ in INPUTS],
        out_specs=[pl.BlockSpec(memory_space=pltpu.VMEM) for _ in OUTPUTS],
        scratch_shapes=[pltpu.VMEM(shape, dtype) for shape, dtype in SCRATCH.values()]
        + [DMA(shape) for shape in SEMAPHORES.values()],
        compiler_params=pltpu.CompilerParams(
            collective_id=0, has_side_effects=True, vmem_limit_bytes=56 * 1024 * 1024
        ),
        name="spectral_layer",
    )(*[jnp.asarray(values[name]) for name in INPUTS])
    return (
        output.reshape(field_in.shape),
        grad_input.reshape(field_in.shape),
        jnp.transpose(grad_spectral, (0, 3, 1, 2)),
        grad_local,
    )


def solution(mesh):
    placed = (
        P(None, "slab", None, None, "gy"),
        P(None, "slab", None, None, "gy"),
        P(None, "slab", None, "gy"),
        P(),
    )
    return jax.shard_map(
        per_device,
        mesh=mesh,
        in_specs=placed,
        out_specs=(
            P(None, "slab", None, None, "gy"),
            P(None, "slab", None, None, "gy"),
            P(None, "slab", None, "gy"),
            P(),
        ),
        check_vma=False,
    )
```

time: 1450 us -> 82.1 us (0.06)
  blocking collectives: 1160 us -> 0 us
  starting transfers between devices: 124 us -> 0 us
  matrix products: 87.6 us -> 0 us
  Pallas kernels: 0 us -> 75.9 us
  local copies, waits for them, and re-layouts: 59.7 us -> 5.43 us
    all_gather x8 -> x0, blocking collectives: 660 us -> none  [the longest x2 260 us: from_modes(): lax.all_gather(spectrum[0], 'slab', axis=0, tiled=True)]
    unnamed x3 -> x0, blocking collectives: 328 us -> none
    psum x3 -> x0, blocking collectives: 173 us -> none  [the longest x1 107 us: per_device(): grad_local = lax.psum(local_terms, ('slab', 'gy')) * forward_scale]
    unnamed x40 -> x0, starting transfers between devices: 124 us -> none
    dot_general x39 -> x0, matrix products: 87.6 us -> none  [the longest x8 20.3 us: rows_forward(): return jnp.einsum('crkq,rp->pkqc', values, table, precision=highest)]
    pallas_call x0 -> x1, Pallas kernels: none -> 75.9 us  [per_device(): pl.pallas_call(layer_kernel, out_shape=[jax.ShapeDtypeStruct(shape, dtype...]
    unnamed x112 -> x10, local copies, waits for them, and re-layouts: 46.6 us -> 5.43 us
  transfers between devices with their start and end apart: 40 -> 0, of which waited for: 1 -> 0; matrix products, arithmetic and copies ran while one was open for 3% -> 0% of each run, Pallas kernels for 0% -> 0%
where the time goes in v3:
time: 82.1 us; the launch traced here: 82 us
  Pallas kernels  75.9 us (92%)
  local copies, waits for them, and re-layouts  5.43 us (7%)
    pallas_call x1, Pallas kernels, per_device(): pl.pallas_call(layer_kernel, out_shape=[jax.ShapeDtypeStruct(shape, dtype...  75.9 us
    unnamed x10, local copies, waits for them, and re-layouts  5.43 us

profile of v3, /device:TPU:1, one launch (start us, length us, event | category | flops | bytes accessed | tf_op | source)
XLA Modules:
  0.0 82.0 jit_solution(15618708101872214725)
XLA Ops:
  0.6 75.9 %spectral_layer.1 = (bf16[32,3,64,128]{3,2,1,0:T(8,128)(2,1)}, bf16[32,3,64,128]{3,2,1,0:T(8,128)(2,1)}, f32[2,32,8,54]{3,2,1,0:T(8,128)}, f32[32,32]{1,0:T(8,128)}) custom-call(bf16[32,3,64,128]{3,2,1,0:T(8,128)(2,1)} %bitcast.6, bf16[32,3,64,128]{3,2,1,0:T(8,128)(2,1)} %bitcast.7, bf16[2,32,8,54]{3,2,1,0:T(8,128)(2,1)} %bitcast.11, ...), custom_call_target="tpu_custom_call" | custom-call | tf_op jit(solution)/shard_map/spectral_layer/pallas_call | solution.py:711
  76.6 0.0 copy-start
  76.6 3.0 %copy.23 = bf16[32,3,2,32,128]{4,3,2,1,0:T(8,128)(2,1)} copy(bf16[32,3,2,32,128]{4,3,2,1,0:T(8,128)(2,1)} %bitcast.9) | data formatting | bytes 3145728
  79.5 0.0 copy-done
  79.6 0.0 copy-start.1
  79.6 0.0 copy-start.2
  79.6 1.1 %copy.24 = bf16[32,3,2,32,128]{4,3,2,1,0:T(8,128)(2,1)} copy(bf16[32,3,2,32,128]{4,3,2,1,0:T(8,128)(2,1)S(1)} %bitcast.8) | data formatting | bytes 3145728
  80.7 0.0 copy-done.1
  80.7 0.7 copy.25
  81.4 0.0 copy-done.2
  81.4 0.6 copy.26
Async XLA Ops:
  76.6 3.0 %copy-start = (bf16[32,3,64,128]{3,2,1,0:T(8,128)(2,1)S(1)}, bf16[32,3,64,128]{3,2,1,0:T(8,128)(2,1)}, u32[]{:S(2)}) copy-start(bf16[32,3,64,128]{3,2,1,0:T(8,128)(2,1)} %get-tuple-element.9) | copy-start | bytes 4718596
  79.6 1.1 %copy-start.1 = (f32[2,32,8,54]{3,2,1,0:T(8,128)S(1)}, f32[2,32,8,54]{3,2,1,0:T(8,128)}, u32[]{:S(2)}) copy-start(f32[2,32,8,54]{3,2,1,0:T(8,128)} %get-tuple-element.10) | copy-start | bytes 331780
  79.6 1.9 %copy-start.2 = (f32[32,32]{1,0:T(8,128)S(1)}, f32[32,32]{1,0:T(8,128)}, u32[]{:S(2)}) copy-start(f32[32,32]{1,0:T(8,128)} %get-tuple-element.19) | copy-start | bytes 12292

commit v4 on v3

--- a/solution.py
+++ b/solution.py
@@ -37,7 +37,6 @@
 ROOT_HALF = 0.7071067811865476
 INV_ROOT_TWO_PI = 0.3989422804014327
 HIGHEST = lax.Precision.HIGHEST
-WINDOW = [(z % 4) * 4 + x * 2 + z // 4 for x in range(2) for z in range(8)]
 PLANE = [(h, c, y) for h in range(2) for c in range(2) for y in range(N_Y) if (h, c, y) != (0, 0, 0)]
 PLANE.sort(key=lambda d: -(2 * d[0] + min(d[2], N_Y - d[2])))
 COLUMN = [(x, z) for x in range(2) for z in range(8) if (x, z) != (0, 0)]
@@ -80,8 +79,8 @@
 
 
 def row_tables():
-    main = [9 * w + j for w in WINDOW for j in range(8)]
-    ninth = [9 * w + 8 for w in WINDOW]
+    main = [9 * w + j for w in range(N_R) for j in range(8)]
+    ninth = [9 * w + 8 for w in range(N_R)]
     pairs = np.array(main + main + ninth + ninth)
     part = np.array([0] * 128 + [1] * 128 + [0] * 16 + [1] * 16)
     y, x, part_in, ky = np.unravel_index(np.arange(288), (N_Y, CX, 2, KY))
@@ -140,9 +139,13 @@
     return [body[:, 0:48], body[:, 48:96], jnp.concatenate([body[:, 96:128], tail], axis=1)]
 
 
+def halves_of(values):
+    high = values.astype(BF16)
+    return high, (values - high.astype(F32)).astype(BF16)
+
+
 def product(rows_ref, first, values):
-    high = values.astype(BF16)
-    low = (values - high.astype(F32)).astype(BF16)
+    high, low = halves_of(values)
     both = dot(rows_ref[first], jnp.concatenate([high, low], axis=1), NN)
     width = values.shape[1]
     return both[:, :width] + both[:, width:] + dot(rows_ref[first + 1], high, NN)
@@ -177,7 +180,7 @@
 
 INPUTS = ["field", "cot", "weight", "lw", "depth", "depth_back", "y_table", "y_back", "rows", "expand", "keep"]
 INPUTS += ["select", "place", "gather", "repeat"]
-OUTPUTS = ["out", "grad_in", "grad_spectral", "grad_local"]
+OUTPUTS = ["out", "grad_cells", "grad_spectral", "hx", "grad_local"]
 SCRATCH = {
     "v_field": ((CX, C, TZ, Y), BF16),
     "v_cot": ((CX, C, TZ, Y), BF16),
@@ -199,7 +202,8 @@
     "cells": ((CX * CHUNKS, 256, 256), BF16),
     "cot_cells": ((CX * CHUNKS, 256, 256), F32),
     "local_part": ((CX * CHUNKS, 256, 256), F32),
-    "acc": ((256, 256), F32),
+    "lsend": ((N_GY, N_Y, *TILE), F32),
+    "lrecv": ((15, *TILE), F32),
     "z_all": ((N_GY, CX, LANES, 256), F32),
     "gsend": ((2, N_GY, N_Y, *BIG), F32),
     "grecv": ((2, 15, *BIG), F32),
@@ -215,7 +219,8 @@
     "rall": ((2, 128, 128), F32),
     "hsend": ((2, N_Y, *BIG), F32),
     "hall": ((2, N_Y, N_GY, *BIG), F32),
-    "hx": ((CX, N_GY, 24, 256), F32),
+    "v_out": ((CX, C, TZ, Y), BF16),
+    "v_grad_spectral": ((2, C, Q, BLOCK), F32),
     "wsend": ((8, 8, 512), F32),
     "wrecv": ((8, 8, 512), F32),
     "esend": ((2, *TILE), F32),
@@ -228,13 +233,30 @@
 SEMAPHORES = {
     "load_sem": (13,),
     "cell_sem": (2, CX),
+    "store_sem": (2 * CX + 1,),
     "plane_sem": (2, 2, 2, 15),
     "column_sem": (2, 2, 2, 15),
     "core_sem": (2, 2),
+    "local_sem": (2, 15),
     "w_sem": (2, 8),
     "e_sem": (2, 2),
     "home_sem": (2, 2, 8),
 }
+
+
+def spectral_rows(hx, y_back, depth_back, spec, x):
+    for pair in range(2):
+        halves = []
+        for q in (2 * pair, 2 * pair + 1):
+            h = hx[x, q, :, 0:LANES]
+            high = h.astype(BF16).astype(F32)
+            stacked = jnp.concatenate([high, high, h - high], axis=0).astype(BF16)
+            u = dot(stacked, y_back[...], TN)
+            halves.append(jnp.concatenate([u[:, :Y], u[:, Y:]], axis=0).astype(BF16))
+        s = dot(depth_back[...], jnp.concatenate(halves, axis=1), NN)
+        for h in range(2):
+            q = 2 * pair + h
+            spec[q * Q : (q + 1) * Q] = s[:, h * Y : (h + 1) * Y].reshape(Q, TZ, Y)
 
 
 def layer_kernel(*refs):
@@ -247,6 +269,9 @@
     turn, half = lax.rem(z, 4), lax.div(z, 4)
     mine = 4 * x_hi + yy
     near = x_lo * 8 + half * 4
+    from_y = lax.rem(turn + 4 - yy, 4)
+    own_window = from_y * 4 + x_lo * 2 + half
+    home = turn == lax.rem(2 * yy, 4)
 
     sources = {
         "depth": ref.depth,
@@ -291,8 +316,9 @@
 
     def column(k):
         d_lo, dz = COLUMN[k]
-        r_to = lax.rem(x_lo + d_lo, 2) * 8 + lax.rem(z + dz, 8)
-        return r_to, {"slab": yy * N_R + r_to}
+        x_to, z_to = lax.rem(x_lo + d_lo, 2), lax.rem(z + dz, 8)
+        w_to = lax.rem(lax.rem(z_to, 4) + 4 - yy, 4) * 4 + x_to * 2 + lax.div(z_to, 4)
+        return w_to, {"slab": yy * N_R + x_to * 8 + z_to}
 
     def across(slab_of):
         found = []
@@ -303,9 +329,9 @@
                 found.append((to_hi, k, to, (to != slab) if d_hi == 0 else None))
         return found
 
-    owners = across(lambda k: k * N_R + near + yy)
-    blocks = across(lambda k: turn * N_R + near + k)
-    at_home = (turn == yy).astype(jnp.int32)
+    owners = across(lambda k: k * N_R + near + lax.rem(yy + k, 4))
+    blocks = across(lambda k: from_y * N_R + near + k)
+    at_home = home.astype(jnp.int32)
 
     def guarded(away, action):
         if away is None:
@@ -354,8 +380,8 @@
     column_to = [column(k) for k in range(15)]
     slot = {d: k for k, d in enumerate(PLANE)}
 
-    def window(r):
-        return pl.ds(pl.multiple_of(r * 8, 8), 8)
+    def window(w):
+        return pl.ds(pl.multiple_of(w * 8, 8), 8)
 
     def send_home(index, source, target):
         sem = ref.home_sem.at[index]
@@ -364,7 +390,7 @@
             guarded(away, copy.start)
             started.append((away, copy))
 
-        @pl.when(turn == yy)
+        @pl.when(home)
         def _():
             target[mine] = source[...]
 
@@ -390,7 +416,7 @@
                 ref.z_all[2 * pair + h, x, :, 0:Y] = part[:LANES]
                 ref.z_all[2 * pair + h, x, :, Y:] = part[LANES:]
 
-    def to_window(index, local, beside_first, beside_second):
+    def to_window(index, beside_first, beside_second):
         table = ref.v_y_table[...]
         gsend, grecv = ref.gsend.at[index], ref.grecv.at[index]
         for g in range(N_GY):
@@ -398,15 +424,13 @@
                 lanes = slice(24 * (4 * (g // 2) + y), 24 * (4 * (g // 2) + y) + 24)
                 rows = [ref.z_all[q, x, lanes, :] for x in range(CX) for q in (g % 2, g % 2 + 2)]
                 piece = dot(table, jnp.concatenate(rows, axis=0).astype(BF16), NT_DIMS)
-                corner = [] if local is None else [local[8 * g : 8 * g + 8, 8 * y : 8 * y + 8]]
-                gsend[g, y] = pack(piece, corner)
+                gsend[g, y] = pack(piece, [])
         if index == 0:
             pl.semaphore_wait(barrier, 30 + 16 - 2 * at_home)
         sem = ref.plane_sem.at[index, 0]
         first = start_all(sem, [(gsend.at[g, y], grecv.at[k], to) for k, (g, y, to) in enumerate(plane_to)])
         beside_first()
         finish(first)
-        block = jnp.zeros((8, 8), F32)
         for dy in range(N_Y):
             total = gsend[gy, yy] if dy == 0 else None
             for d_hi in range(2):
@@ -414,15 +438,13 @@
                     if (d_hi, d_core, dy) in slot:
                         term = grecv[slot[d_hi, d_core, dy]]
                         total = term if total is None else total + term
-            block = block + total[24:32, 48:56]
             base = lax.rem(yy + N_Y - dy, N_Y) * ROWS
             for x, piece in enumerate(unpack(total)):
                 ref.g12[pl.ds(pl.multiple_of(base + 24 * x, 8), 24), 0:48] = piece
 
         f = product(ref.v_rows, 0, ref.g12[:, 0:48])
         msend, mrecv = ref.msend.at[index], ref.mrecv.at[index]
-        blank = jnp.zeros((128, 24), F32)
-        msend[...] = jnp.concatenate([f[0:128], f[128:256], blank, jnp.concatenate([block] * N_R, axis=0)], axis=1)
+        msend[...] = jnp.concatenate([f[0:128], f[128:256], jnp.zeros((128, 32), F32)], axis=1)
         ninth = jnp.concatenate([f[256:272], f[272:288]], axis=1)
         for j in range(4):
             old = msend[pl.ds(j, N_R, stride=8), :]
@@ -430,47 +452,54 @@
                 [old[:, 0:96], ninth[:, 24 * j : 24 * j + 24], old[:, 120:128]], axis=1
             )
         sem = ref.column_sem.at[index, 0]
-        second = start_all(sem, [(msend.at[window(r)], mrecv.at[k], to) for k, (r, to) in enumerate(column_to)])
+        second = start_all(sem, [(msend.at[window(w)], mrecv.at[k], to) for k, (w, to) in enumerate(column_to)])
         beside_second()
         finish(second)
-        m = msend[window(rr), :]
+        m = msend[window(own_window), :]
         for k in range(15):
             m = m + mrecv[k]
 
         last = jnp.concatenate([m[j : j + 1, 96:120] for j in range(4)], axis=1)
         nine = jnp.concatenate([m[:, 0:96], last, jnp.zeros((7, 96), F32)], axis=0)
-        spread = dot(nine, ref.v_expand[...], TN, HIGHEST) * ref.v_keep[...]
+        expand = ref.v_expand[...].astype(BF16)
+        high, low = halves_of(nine)
+        spread = dot(jnp.concatenate([high, low], axis=0), jnp.concatenate([expand, expand], axis=0), TN)
+        spread = spread * ref.v_keep[...]
         parts = {}
         for n in range(4):
             base = 24 * n
             total = spread[base : base + 8] + spread[base + 8 : base + 16] + spread[base + 16 : base + 24]
             parts[n // 2, n % 2] = total[:, 0:OWN]
-        return parts, m[:, 120:128]
+        return parts
 
     def packed(parts):
         end = jnp.zeros((Q, 128 - 4 * OWN), F32)
         return jnp.concatenate([parts[part, h] for h in range(2) for part in range(2)] + [end], axis=1)
 
-    def from_mixed(index, mixed, corner, beside_first, beside_second):
+    def from_mixed(index, mixed, local, beside_first, beside_second):
         pad = jnp.zeros((Q, 128 - OWN), F32)
         wide = [jnp.concatenate([mixed[part, h], pad], axis=1) for part in range(2) for h in range(2)]
         tiled = jnp.concatenate([v for v in wide for _ in range(3)], axis=0) * ref.v_keep[...]
-        u = dot(ref.v_expand[...], tiled, NT_DIMS, HIGHEST)
+        expand = ref.v_expand[...].astype(BF16)
+        u = dot(jnp.concatenate([expand, expand], axis=1), jnp.concatenate(halves_of(tiled), axis=1), NT_DIMS)
         last = jnp.concatenate([u[8:9, 24 * j : 24 * j + 24] for j in range(4)] + [jnp.zeros((4, 24), F32)], axis=0)
         rsend, rall = ref.rsend.at[index], ref.rall.at[index]
-        rsend[...] = jnp.concatenate([u[0:8], last, jnp.zeros((8, 8), F32)], axis=1)
-        rall[window(rr), :] = rsend[...]
+        rsend[...] = jnp.concatenate([u[0:8], last, local], axis=1)
+        rall[window(own_window), :] = rsend[...]
         sem = ref.column_sem.at[index, 1]
-        third = start_all(sem, [(rsend, rall.at[window(rr)], to) for _, to in column_to])
+        third = start_all(sem, [(rsend, rall.at[window(own_window)], to) for _, to in column_to])
         beside_first()
         finish(third)
         ninth = jnp.concatenate([rall[pl.ds(j, N_R, stride=8), :][:, 96:120] for j in range(4)], axis=1)
         f = jnp.concatenate([rall[:, 0:48], rall[:, 48:96], ninth[:, 0:48], ninth[:, 48:96]], axis=0)
         h = product(ref.v_rows, 2, f)
+        local = rall[0:8, 120:128]
+        for w in range(1, N_R):
+            local = local + rall[8 * w : 8 * w + 8, 120:128]
         hsend, hall = ref.hsend.at[index], ref.hall.at[index]
         for y in range(N_Y):
             rows = [h[y * ROWS + 24 * x : y * ROWS + 24 * x + 24] for x in range(CX)]
-            hsend[y] = pack(jnp.concatenate(rows, axis=1), corner)
+            hsend[y] = pack(jnp.concatenate(rows, axis=1), [local])
         hall[yy, gy] = hsend[yy]
         sem = ref.plane_sem.at[index, 1]
         fourth = start_all(sem, [(hsend.at[y], hall.at[yy, gy], to) for _, y, to in plane_to])
@@ -482,20 +511,6 @@
                 for x, piece in enumerate(unpack(hall[y, g])):
                     for h in range(2):
                         ref.hx[x, 2 * h + g % 2, :, base : base + 24] = piece[:, 24 * h : 24 * h + 24]
-
-    def spectral_rows(x):
-        for pair in range(2):
-            halves = []
-            for q in (2 * pair, 2 * pair + 1):
-                h = ref.hx[x, q, :, 0:LANES]
-                high = h.astype(BF16).astype(F32)
-                stacked = jnp.concatenate([high, high, h - high], axis=0).astype(BF16)
-                u = dot(stacked, ref.v_y_back[...], TN)
-                halves.append(jnp.concatenate([u[:, :Y], u[:, Y:]], axis=0).astype(BF16))
-            s = dot(ref.v_depth_back[...], jnp.concatenate(halves, axis=1), NN)
-            for h in range(2):
-                q = 2 * pair + h
-                ref.spec[q * Q : (q + 1) * Q] = s[:, h * Y : (h + 1) * Y].reshape(Q, TZ, Y)
 
     ready("depth", "y_table")
     for x in range(CX):
@@ -520,7 +535,7 @@
             started.append((away, copy))
         for e in range(2):
             to_hi, y = lax.div(turn, 2), lax.rem(2 * turn, 4) + e
-            to = y * N_R + near + yy
+            to = y * N_R + near + lax.rem(yy + y, 4)
             copy = copy_to(
                 ref.esend.at[e], ref.erecv.at[x_hi], ref.e_sem.at[0, e], ref.e_sem.at[1, x_hi], device_of(to_hi, to)
             )
@@ -533,7 +548,7 @@
             def _():
                 ref.erecv[x_hi] = ref.esend[e]
 
-        @pl.when(turn == yy)
+        @pl.when(home)
         def _():
             ref.wrecv[own] = ref.wsend[mine]
 
@@ -546,7 +561,7 @@
                 ref.wsend.at[0], ref.wrecv.at[at], ref.w_sem.at[0, k], ref.w_sem.at[1, at], device_of(from_hi, origin)
             )
             guarded(away, copy.wait_recv)
-        origin = turn * N_R + near + lax.div(mine, 2)
+        origin = from_y * N_R + near + lax.div(mine, 2)
         for hi in range(2):
             copy = copy_to(
                 ref.esend.at[0], ref.erecv.at[hi], ref.e_sem.at[0, hi], ref.e_sem.at[1, hi], device_of(hi, origin)
@@ -556,10 +571,10 @@
         received = jnp.concatenate([ref.wrecv[...].reshape(64, 512), *ninths, jnp.zeros((6, 512), F32)], axis=0)
         ref.owned[...] = dot(received.astype(BF16), ref.v_place[...].astype(BF16), TN)
 
-    def local_products(weight_transposed, cells_of):
-        kron = channel_matrix(ref.v_lw[...], ref.v_repeat[...], weight_transposed)
+    def local_products():
+        kron = channel_matrix(ref.v_lw[...], ref.v_repeat[...], True)
         for n in range(CX * CHUNKS):
-            ref.local_part[n] = dot(kron, cells_of(n), NN)
+            ref.local_part[n] = dot(kron, ref.cells[n], NN)
 
     def prepare_cells():
         ready("lw", "repeat", "depth_back", "y_back", "gather")
@@ -575,7 +590,7 @@
         receive_weights()
         prepare_cells()
 
-    parts, _ = to_window(0, None, send_weights, beside_column)
+    parts = to_window(0, send_weights, beside_column)
 
     other_core = {"gy": x_hi * 2 + 1 - core}
     ref.qbuf[core] = packed(parts)
@@ -603,17 +618,23 @@
 
     def beside_modes():
         send_home(0, ref.qbuf, ref.home_modes)
-        local_products(True, lambda n: ref.cells[n])
+        local_products()
 
     def modes_home():
         come_home(0, ref.qbuf, ref.home_modes)
         ref.block_modes[...] = in_block_order([ref.home_modes[k].reshape(16, 128) for k in range(8)])
 
-    from_mixed(0, mixed, [], beside_modes, modes_home)
-
-    ref.acc[...] = jnp.zeros_like(ref.acc)
+    from_mixed(0, mixed, jnp.zeros((8, 8), F32), beside_modes, modes_home)
+
+    stores = []
+
+    def store(source, target):
+        copy = pltpu.make_async_copy(source, target, ref.store_sem.at[len(stores)])
+        copy.start()
+        stores.append(copy)
+
     for x in range(CX):
-        spectral_rows(x)
+        spectral_rows(ref.hx, ref.v_y_back, ref.v_depth_back, ref.spec, x)
         for r in range(CHUNKS):
             n = x * CHUNKS + r
             rows = slice(16 * r, 16 * r + 16)
@@ -621,19 +642,28 @@
             cdf = 0.5 * (1.0 + lax.erf(pre * ROOT_HALF))
             slope = cdf + pre * jnp.exp(-0.5 * pre * pre) * INV_ROOT_TWO_PI
             grad = ref.cot_cells[n] * slope
-            ref.out[:, x, rows, :] = unchunk(pre * cdf).astype(BF16)
+            ref.v_out[x, :, rows, :] = unchunk(pre * cdf).astype(BF16)
             ref.grad_pre[x, :, rows, :] = unchunk(grad).astype(BF16)
-            ref.acc[...] += dot(ref.cells[n], grad.astype(BF16), NT_DIMS)
+        store(ref.v_out.at[x], ref.out.at[:, x])
+        store(ref.grad_pre.at[x], ref.grad_cells.at[:, x])
         depth_stage(lambda x, c: ref.grad_pre[x, c], x)
-    kept = jnp.where(same_row((256, 256)), ref.acc[...], 0.0)
-    repeat = ref.v_repeat[...].astype(F32)
-    local = dot(dot(repeat, kept, TN, HIGHEST), repeat, NN, HIGHEST)
-
-    def chunk_grad(n):
-        x, r = divmod(n, CHUNKS)
-        return chunk_of(ref.grad_pre[x, :, 16 * r : 16 * r + 16, :]).astype(BF16)
-
-    parts, total_local = to_window(1, local, lambda: None, lambda: local_products(False, chunk_grad))
+    def local_terms():
+        total = jnp.zeros((256, 256), F32)
+        for n in range(CX * CHUNKS):
+            x, r = divmod(n, CHUNKS)
+            grad = chunk_of(ref.grad_pre[x, :, 16 * r : 16 * r + 16, :]).astype(BF16)
+            total = total + dot(ref.cells[n], grad, NT_DIMS)
+        kept = jnp.where(same_row((256, 256)), total, 0.0)
+        repeat = ref.v_repeat[...].astype(F32)
+        local = dot(dot(repeat, kept, TN, HIGHEST), repeat, NN, HIGHEST)
+        for g in range(N_GY):
+            for y in range(N_Y):
+                ref.lsend[g, y, :, 0:8] = local[8 * g : 8 * g + 8, 8 * y : 8 * y + 8]
+        copies = [(ref.lsend.at[g, y], ref.lrecv.at[k], to) for k, (g, y, to) in enumerate(plane_to)]
+        local_copies.extend(start_all(ref.local_sem, copies))
+
+    local_copies = []
+    parts = to_window(1, local_terms, lambda: None)
     ref.grads[...] = packed(parts)
     gr, gi = (jnp.concatenate([parts[p, 0], parts[p, 1]], axis=1) for p in range(2))
     for i in range(C):
@@ -664,22 +694,66 @@
             q, c = divmod(i, Q)
             row = 32 * (q // 2) + 8 * (q % 2) + c
             mr, mi = ref.block_modes[row : row + 1, 0:BLOCK], ref.block_modes[row + 16 : row + 17, 0:BLOCK]
-            ref.grad_spectral[0, i] = mr * gr + mi * gi
-            ref.grad_spectral[1, i] = mr * gi - mi * gr
-
-    from_mixed(1, mixed, [total_local], lambda: send_home(1, ref.grads, ref.home_grads), weight_gradient)
+            ref.v_grad_spectral[0, i] = mr * gr + mi * gi
+            ref.v_grad_spectral[1, i] = mr * gi - mi * gr
+        store(ref.v_grad_spectral, ref.grad_spectral)
+
+    finish(local_copies)
+    local = ref.lsend[gy, yy, :, 0:8]
+    for k in range(15):
+        local = local + ref.lrecv[k, :, 0:8]
+    from_mixed(1, mixed, local, lambda: send_home(1, ref.grads, ref.home_grads), weight_gradient)
     for y in range(N_Y):
         for g in range(N_GY):
             corner = ref.hall[1, y, g, 24:32, 48:56]
             ref.grad_local[8 * g : 8 * g + 8, 8 * y : 8 * y + 8] = corner * FORWARD_SCALE
+    for copy in stores:
+        copy.wait()
+    for away, copy in started:
+        guarded(away, copy.wait_send)
+
+
+def last_kernel(
+    grad_cells, hx, early_out, early_spectral, early_local, lw, repeat, y_back, depth_back,
+    out, grad_in, grad_spectral, grad_local,
+    v_hx, v_cells, v_lw, v_repeat, v_y_back, v_depth_back, v_out, spec, v_pass, v_spectral, v_local, sem, pass_sem, store_sem,
+):
+    gy = lax.axis_index("gy")
+    staged = [
+        (hx, v_hx),
+        (y_back.at[gy], v_y_back),
+        (depth_back, v_depth_back),
+        (lw, v_lw),
+        (repeat, v_repeat),
+        *[(grad_cells.at[:, x], v_cells.at[x]) for x in range(CX)],
+    ]
+    loads = [pltpu.make_async_copy(a, b, sem.at[k]) for k, (a, b) in enumerate(staged)]
+    passed = [(early_out, v_pass, out), (early_spectral, v_spectral, grad_spectral), (early_local, v_local, grad_local)]
+    arrive = [pltpu.make_async_copy(a, b, pass_sem.at[0, k]) for k, (a, b, _) in enumerate(passed)]
+    leave = [pltpu.make_async_copy(b, c, pass_sem.at[1, k]) for k, (_, b, c) in enumerate(passed)]
+    for copy in loads + arrive:
+        copy.start()
+    for copy in loads[:5]:
+        copy.wait()
+    kron = channel_matrix(v_lw[...], v_repeat[...], False)
+    stores = []
     for x in range(CX):
-        spectral_rows(x)
+        spectral_rows(v_hx, v_y_back, v_depth_back, spec, x)
+        if x == 0:
+            for first, second in zip(arrive, leave):
+                first.wait()
+                second.start()
+        loads[5 + x].wait()
         for r in range(CHUNKS):
             rows = slice(16 * r, 16 * r + 16)
-            total = chunk_of(ref.spec[:, rows, :]) + ref.local_part[x * CHUNKS + r]
-            ref.grad_in[:, x, rows, :] = unchunk(total).astype(BF16)
-    for away, copy in started:
-        guarded(away, copy.wait_send)
+            cells = chunk_of(v_cells[x, :, rows, :]).astype(BF16)
+            total = chunk_of(spec[:, rows, :]) + dot(kron, cells, NN)
+            v_out[x, :, rows, :] = unchunk(total).astype(BF16)
+        copy = pltpu.make_async_copy(v_out.at[x], grad_in.at[:, x], store_sem.at[x])
+        copy.start()
+        stores.append(copy)
+    for copy in leave + stores:
+        copy.wait()
 
 
 def per_device(field_in, cotangent, spectral_weight, local_weight):
@@ -707,19 +781,44 @@
         "gather": gather.astype(np.float32),
         "repeat": np.repeat(np.eye(C), 8, axis=0).astype(BF16),
     }
-    outs = [(cells, BF16), (cells, BF16), ((2, C, Q, BLOCK), F32), ((C, C), F32)]
-    output, grad_input, grad_spectral, grad_local = pl.pallas_call(
+    values = {name: jnp.asarray(value) for name, value in values.items()}
+    vmem, anywhere = pl.BlockSpec(memory_space=pltpu.VMEM), pl.BlockSpec(memory_space=pl.ANY)
+    field, mixed, local = ((cells, BF16), ((2, C, Q, BLOCK), F32), ((C, C), F32))
+    outs = [field, field, mixed, ((CX, N_GY, 24, 256), F32), local]
+    early_out, grad_cells, early_spectral, hx, early_local = pl.pallas_call(
         layer_kernel,
         out_shape=[jax.ShapeDtypeStruct(shape, dtype) for shape, dtype in outs],
-        in_specs=[pl.BlockSpec(memory_space=pltpu.HBM) for _ in INPUTS],
-        out_specs=[pl.BlockSpec(memory_space=pltpu.VMEM) for _ in OUTPUTS],
+        in_specs=[anywhere for _ in INPUTS],
+        out_specs=[anywhere] * 3 + [vmem] * 2,
         scratch_shapes=[pltpu.VMEM(shape, dtype) for shape, dtype in SCRATCH.values()]
         + [DMA(shape) for shape in SEMAPHORES.values()],
         compiler_params=pltpu.CompilerParams(
             collective_id=0, has_side_effects=True, vmem_limit_bytes=56 * 1024 * 1024
         ),
         name="spectral_layer",
-    )(*[jnp.asarray(values[name]) for name in INPUTS])
+    )(*[values[name] for name in INPUTS])
+    output, grad_input, grad_spectral, grad_local = pl.pallas_call(
+        last_kernel,
+        out_shape=[jax.ShapeDtypeStruct(shape, dtype) for shape, dtype in (field, field, mixed, local)],
+        in_specs=[anywhere] * 9,
+        out_specs=[anywhere] * 4,
+        scratch_shapes=[
+            pltpu.VMEM((CX, N_GY, 24, 256), F32),
+            pltpu.VMEM((CX, C, TZ, Y), BF16),
+            pltpu.VMEM((C, C), BF16),
+            pltpu.VMEM((256, C), BF16),
+            pltpu.VMEM((6 * KY, 2 * Y), BF16),
+            pltpu.VMEM((Q * TZ, 2 * K * Q), BF16),
+            pltpu.VMEM((CX, C, TZ, Y), BF16),
+            pltpu.VMEM((C, TZ, Y), F32),
+            *[pltpu.VMEM(shape, dtype) for shape, dtype in (field, mixed, local)],
+            DMA((8,)),
+            DMA((2, 3)),
+            DMA((CX,)),
+        ],
+        compiler_params=pltpu.CompilerParams(vmem_limit_bytes=56 * 1024 * 1024),
+        name="last_cells",
+    )(grad_cells, hx, early_out, early_spectral, early_local, *[values[n] for n in ("lw", "repeat", "y_back", "depth_back")])
     return (
         output.reshape(field_in.shape),
         grad_input.reshape(field_in.shape),

time: 82.1 us -> 78.2 us (0.952)
  local copies, waits for them, and re-layouts: 5.43 us -> 0 us
  Pallas kernels: 75.9 us -> 77.3 us
    unnamed x10 -> x0, local copies, waits for them, and re-layouts: 5.43 us -> none
    pallas_call x0 -> x1, Pallas kernels: none -> 5.06 us  [per_device(): pl.pallas_call(last_kernel, out_shape=[jax.ShapeDtypeStruct(shape, dtype)...]
    pallas_call x1, Pallas kernels: 75.9 us -> 72.2 us  [per_device(): pl.pallas_call(layer_kernel, out_shape=[jax.ShapeDtypeStruct(shape, dtype...]
where the time goes in v4:
time: 78.2 us; the launch traced here: 78.1 us
  Pallas kernels  77.3 us (99%)
  between operations  0.8 us (1%)
    pallas_call x1, Pallas kernels, per_device(): pl.pallas_call(layer_kernel, out_shape=[jax.ShapeDtypeStruct(shape, dtype...  72.2 us
    pallas_call x1, Pallas kernels, per_device(): pl.pallas_call(last_kernel, out_shape=[jax.ShapeDtypeStruct(shape, dtype)...  5.06 us

profile of v4, /device:TPU:1, one launch (start us, length us, event | category | flops | bytes accessed | tf_op | source)
XLA Modules:
  0.0 78.1 jit_solution(12972639809595769795)
XLA Ops:
  0.6 72.2 %spectral_layer.1 = (bf16[32,3,64,128]{3,2,1,0:T(8,128)(2,1)}, bf16[32,3,64,128]{3,2,1,0:T(8,128)(2,1)}, f32[2,32,8,54]{3,2,1,0:T(8,128)}, f32[3,4,24,256]{3,2,1,0:T(8,128)}, f32[32,32]{1,0:T(8,128)}) custom-call(bf16[32,3,64,128]{3,2,1,0:T(8,128)(2,1)} %bitcast.6, bf16[32,3,64,128]{3,2,1,0:T(8,128)(2,1)} %bitcast.7, bf16[2,32,8,54]{3,2,1,0:T(8,128)(2,1)} %bitcast.8, ...), custom_call_target="tpu_custom_call" | custom-call | tf_op jit(solution)/shard_map/spectral_layer/pallas_call | solution.py:788
  72.9 5.1 %last_cells.1 = (bf16[32,3,64,128]{3,2,1,0:T(8,128)(2,1)}, bf16[32,3,64,128]{3,2,1,0:T(8,128)(2,1)}, f32[2,32,8,54]{3,2,1,0:T(8,128)}, f32[32,32]{1,0:T(8,128)}) custom-call(bf16[32,3,64,128]{3,2,1,0:T(8,128)(2,1)} %get-tuple-element.13.grad_cells, f32[3,4,24,256]{3,2,1,0:T(8,128)} %get-tuple-element.14.hx, ...), custom_call_target="tpu_custom_call" | custom-call | tf_op jit(solution)/shard_map/last_cells/pallas_call | solution.py:800

commit v5 on v4

--- a/solution.py
+++ b/solution.py
@@ -38,9 +38,9 @@
 INV_ROOT_TWO_PI = 0.3989422804014327
 HIGHEST = lax.Precision.HIGHEST
 PLANE = [(h, c, y) for h in range(2) for c in range(2) for y in range(N_Y) if (h, c, y) != (0, 0, 0)]
-PLANE.sort(key=lambda d: -(2 * d[0] + min(d[2], N_Y - d[2])))
+PLANE.sort(key=lambda d: -(3 * d[0] + min(d[2], N_Y - d[2])))
 COLUMN = [(x, z) for x in range(2) for z in range(8) if (x, z) != (0, 0)]
-COLUMN.sort(key=lambda d: -(d[0] + min(d[1], 8 - d[1])))
+COLUMN.sort(key=lambda d: -(0.5 * d[0] + min(d[1], 8 - d[1])))
 F32 = jnp.float32
 BF16 = jnp.bfloat16
 MESH = pl.DeviceIdType.MESH
@@ -198,7 +198,7 @@
     "v_gather": ((8 * OWN, 128), F32),
     "v_repeat": ((256, C), BF16),
     "grad_pre": ((CX, C, TZ, Y), BF16),
-    "spec": ((C, TZ, Y), F32),
+    "spec": ((CX, C, TZ, Y), F32),
     "cells": ((CX * CHUNKS, 256, 256), BF16),
     "cot_cells": ((CX * CHUNKS, 256, 256), F32),
     "local_part": ((CX * CHUNKS, 256, 256), F32),
@@ -376,6 +376,11 @@
         for copy in made:
             copy.wait_recv()
 
+    def drain(count):
+        for away, copy in started[:count]:
+            guarded(away, copy.wait_send)
+        del started[:count]
+
     plane_to = [plane(k) for k in range(15)]
     column_to = [column(k) for k in range(15)]
     slot = {d: k for k, d in enumerate(PLANE)}
@@ -419,12 +424,11 @@
     def to_window(index, beside_first, beside_second):
         table = ref.v_y_table[...]
         gsend, grecv = ref.gsend.at[index], ref.grecv.at[index]
-        for g in range(N_GY):
-            for y in range(N_Y):
-                lanes = slice(24 * (4 * (g // 2) + y), 24 * (4 * (g // 2) + y) + 24)
-                rows = [ref.z_all[q, x, lanes, :] for x in range(CX) for q in (g % 2, g % 2 + 2)]
-                piece = dot(table, jnp.concatenate(rows, axis=0).astype(BF16), NT_DIMS)
-                gsend[g, y] = pack(piece, [])
+        for c in range(2):
+            rows = [ref.z_all[q, x, 24 * p : 24 * p + 24, :] for p in range(8) for x in range(CX) for q in (c, c + 2)]
+            wide = dot(table, jnp.concatenate(rows, axis=0).astype(BF16), NT_DIMS)
+            for p in range(8):
+                gsend[2 * (p // 4) + c, p % 4] = pack(wide[:, 144 * p : 144 * p + 144], [])
         if index == 0:
             pl.semaphore_wait(barrier, 30 + 16 - 2 * at_home)
         sem = ref.plane_sem.at[index, 0]
@@ -452,7 +456,9 @@
                 [old[:, 0:96], ninth[:, 24 * j : 24 * j + 24], old[:, 120:128]], axis=1
             )
         sem = ref.column_sem.at[index, 0]
+        before = len(started)
         second = start_all(sem, [(msend.at[window(w)], mrecv.at[k], to) for k, (w, to) in enumerate(column_to)])
+        drain(before)
         beside_second()
         finish(second)
         m = msend[window(own_window), :]
@@ -487,7 +493,9 @@
         rsend[...] = jnp.concatenate([u[0:8], last, local], axis=1)
         rall[window(own_window), :] = rsend[...]
         sem = ref.column_sem.at[index, 1]
+        before = len(started)
         third = start_all(sem, [(rsend, rall.at[window(own_window)], to) for _, to in column_to])
+        drain(before)
         beside_first()
         finish(third)
         ninth = jnp.concatenate([rall[pl.ds(j, N_R, stride=8), :][:, 96:120] for j in range(4)], axis=1)
@@ -502,7 +510,9 @@
             hsend[y] = pack(jnp.concatenate(rows, axis=1), [local])
         hall[yy, gy] = hsend[yy]
         sem = ref.plane_sem.at[index, 1]
+        before = len(started)
         fourth = start_all(sem, [(hsend.at[y], hall.at[yy, gy], to) for _, y, to in plane_to])
+        drain(before)
         beside_second()
         finish(fourth)
         for y in range(N_Y):
@@ -634,11 +644,12 @@
         stores.append(copy)
 
     for x in range(CX):
-        spectral_rows(ref.hx, ref.v_y_back, ref.v_depth_back, ref.spec, x)
+        spectral_rows(ref.hx, ref.v_y_back, ref.v_depth_back, ref.spec.at[x], x)
+    for x in range(CX):
         for r in range(CHUNKS):
             n = x * CHUNKS + r
             rows = slice(16 * r, 16 * r + 16)
-            pre = chunk_of(ref.spec[:, rows, :]) + ref.local_part[n]
+            pre = chunk_of(ref.spec[x, :, rows, :]) + ref.local_part[n]
             cdf = 0.5 * (1.0 + lax.erf(pre * ROOT_HALF))
             slope = cdf + pre * jnp.exp(-0.5 * pre * pre) * INV_ROOT_TWO_PI
             grad = ref.cot_cells[n] * slope
@@ -709,8 +720,7 @@
             ref.grad_local[8 * g : 8 * g + 8, 8 * y : 8 * y + 8] = corner * FORWARD_SCALE
     for copy in stores:
         copy.wait()
-    for away, copy in started:
-        guarded(away, copy.wait_send)
+    drain(len(started))
 
 
 def last_kernel(

time: 78.2 us -> 77.4 us (0.990)
  Pallas kernels: 77.3 us -> 76.5 us
    pallas_call x1, Pallas kernels: 72.2 us -> 71.4 us  [per_device(): pl.pallas_call(layer_kernel, out_shape=[jax.ShapeDtypeStruct(shape, dtype...]
where the time goes in v5:
time: 77.4 us; the launch traced here: 77.3 us
  Pallas kernels  76.5 us (99%)
  between operations  0.8 us (1%)
    pallas_call x1, Pallas kernels, per_device(): pl.pallas_call(layer_kernel, out_shape=[jax.ShapeDtypeStruct(shape, dtype...  71.4 us
    pallas_call x1, Pallas kernels, per_device(): pl.pallas_call(last_kernel, out_shape=[jax.ShapeDtypeStruct(shape, dtype)...  5.06 us

profile of v5, /device:TPU:1, one launch (start us, length us, event | category | flops | bytes accessed | tf_op | source)
XLA Modules:
  0.0 77.3 jit_solution(9860804150853977366)
XLA Ops:
  0.6 71.4 %spectral_layer.1 = (bf16[32,3,64,128]{3,2,1,0:T(8,128)(2,1)}, bf16[32,3,64,128]{3,2,1,0:T(8,128)(2,1)}, f32[2,32,8,54]{3,2,1,0:T(8,128)}, f32[3,4,24,256]{3,2,1,0:T(8,128)}, f32[32,32]{1,0:T(8,128)}) custom-call(bf16[32,3,64,128]{3,2,1,0:T(8,128)(2,1)} %bitcast.6, bf16[32,3,64,128]{3,2,1,0:T(8,128)(2,1)} %bitcast.7, bf16[2,32,8,54]{3,2,1,0:T(8,128)(2,1)} %bitcast.8, ...), custom_call_target="tpu_custom_call" | custom-call | tf_op jit(solution)/shard_map/spectral_layer/pallas_call | solution.py:798
  72.0 5.1 %last_cells.1 = (bf16[32,3,64,128]{3,2,1,0:T(8,128)(2,1)}, bf16[32,3,64,128]{3,2,1,0:T(8,128)(2,1)}, f32[2,32,8,54]{3,2,1,0:T(8,128)}, f32[32,32]{1,0:T(8,128)}) custom-call(bf16[32,3,64,128]{3,2,1,0:T(8,128)(2,1)} %get-tuple-element.13.grad_cells, f32[3,4,24,256]{3,2,1,0:T(8,128)} %get-tuple-element.14.hx, ...), custom_call_target="tpu_custom_call" | custom-call | tf_op jit(solution)/shard_map/last_cells/pallas_call | solution.py:810

commit v6 on v5

--- a/solution.py
+++ b/solution.py
@@ -184,12 +184,12 @@
 SCRATCH = {
     "v_field": ((CX, C, TZ, Y), BF16),
     "v_cot": ((CX, C, TZ, Y), BF16),
-    "v_weight": ((2, C, Q, BLOCK), BF16),
+    "v_weight": ((2 * C * Q, BLOCK), BF16),
     "v_lw": ((C, C), BF16),
     "v_depth": ((2 * K * Q, Q * TZ), BF16),
     "v_depth_back": ((Q * TZ, 2 * K * Q), BF16),
-    "v_y_table": ((2 * KY, 2 * Y), BF16),
-    "v_y_back": ((6 * KY, 2 * Y), BF16),
+    "v_y_table": ((32, 2 * Y), BF16),
+    "v_y_back": ((80, 2 * Y), BF16),
     "v_rows": ((4, 288, 288), BF16),
     "v_expand": ((16, 128), F32),
     "v_keep": ((96, 128), F32),
@@ -208,7 +208,7 @@
     "gsend": ((2, N_GY, N_Y, *BIG), F32),
     "grecv": ((2, 15, *BIG), F32),
     "g12": ((288, 128), F32),
-    "msend": ((2, 128, 128), F32),
+    "msend": ((2, 136, 128), F32),
     "mrecv": ((2, 15, *TILE), F32),
     "qbuf": ((2, *TILE), F32),
     "qsend": ((2, *TILE), F32),
@@ -216,7 +216,7 @@
     "sums": ((N_GY, 16, 128), F32),
     "grads": (TILE, F32),
     "rsend": ((2, *TILE), F32),
-    "rall": ((2, 128, 128), F32),
+    "rall": ((2, 136, 128), F32),
     "hsend": ((2, N_Y, *BIG), F32),
     "hall": ((2, N_Y, N_GY, *BIG), F32),
     "v_out": ((CX, C, TZ, Y), BF16),
@@ -250,7 +250,7 @@
         for q in (2 * pair, 2 * pair + 1):
             h = hx[x, q, :, 0:LANES]
             high = h.astype(BF16).astype(F32)
-            stacked = jnp.concatenate([high, high, h - high], axis=0).astype(BF16)
+            stacked = jnp.concatenate([high, high, h - high, jnp.zeros((8, LANES), F32)], axis=0).astype(BF16)
             u = dot(stacked, y_back[...], TN)
             halves.append(jnp.concatenate([u[:, :Y], u[:, Y:]], axis=0).astype(BF16))
         s = dot(depth_back[...], jnp.concatenate(halves, axis=1), NN)
@@ -426,7 +426,7 @@
         gsend, grecv = ref.gsend.at[index], ref.grecv.at[index]
         for c in range(2):
             rows = [ref.z_all[q, x, 24 * p : 24 * p + 24, :] for p in range(8) for x in range(CX) for q in (c, c + 2)]
-            wide = dot(table, jnp.concatenate(rows, axis=0).astype(BF16), NT_DIMS)
+            wide = dot(table, jnp.concatenate(rows, axis=0).astype(BF16), NT_DIMS)[0 : 2 * KY]
             for p in range(8):
                 gsend[2 * (p // 4) + c, p % 4] = pack(wide[:, 144 * p : 144 * p + 144], [])
         if index == 0:
@@ -448,7 +448,7 @@
 
         f = product(ref.v_rows, 0, ref.g12[:, 0:48])
         msend, mrecv = ref.msend.at[index], ref.mrecv.at[index]
-        msend[...] = jnp.concatenate([f[0:128], f[128:256], jnp.zeros((128, 32), F32)], axis=1)
+        msend[0:128, :] = jnp.concatenate([f[0:128], f[128:256], jnp.zeros((128, 32), F32)], axis=1)
         ninth = jnp.concatenate([f[256:272], f[272:288]], axis=1)
         for j in range(4):
             old = msend[pl.ds(j, N_R, stride=8), :]
@@ -499,7 +499,7 @@
         beside_first()
         finish(third)
         ninth = jnp.concatenate([rall[pl.ds(j, N_R, stride=8), :][:, 96:120] for j in range(4)], axis=1)
-        f = jnp.concatenate([rall[:, 0:48], rall[:, 48:96], ninth[:, 0:48], ninth[:, 48:96]], axis=0)
+        f = jnp.concatenate([rall[0:128, 0:48], rall[0:128, 48:96], ninth[:, 0:48], ninth[:, 48:96]], axis=0)
         h = product(ref.v_rows, 2, f)
         local = rall[0:8, 120:128]
         for w in range(1, N_R):
@@ -529,8 +529,7 @@
 
     def send_weights():
         ready("weight", "select", "place")
-        flat = ref.v_weight[...].astype(F32).reshape(2 * C * Q, BLOCK).astype(BF16)
-        picked = dot(ref.v_select[...][:, 0:BLOCK].astype(BF16), flat, NT_DIMS)
+        picked = dot(ref.v_select[...][:, 0:BLOCK].astype(BF16), ref.v_weight[...], NT_DIMS)
         for k in range(8):
             ref.wsend[k] = picked[8 * k : 8 * k + 8]
         for e in range(2):
@@ -772,17 +771,18 @@
     tables = y_tables()
     high = tables.astype(BF16)
     low = (tables - high.astype(np.float64)).astype(BF16)
+    blank = np.zeros((N_GY, 8, 2 * Y), BF16)
     expand, keep = unit_tables()
     select, place, gather = owner_tables()
     values = {
         "field": field_in.reshape(cells),
         "cot": cotangent.reshape(cells),
-        "weight": jnp.transpose(spectral_weight, (0, 2, 3, 1)),
+        "weight": jnp.transpose(spectral_weight, (0, 2, 3, 1)).reshape(2 * C * Q, BLOCK),
         "lw": local_weight,
         "depth": depth.astype(BF16),
         "depth_back": np.ascontiguousarray(depth.T).astype(BF16),
-        "y_table": high,
-        "y_back": np.concatenate([high, low, high], axis=1),
+        "y_table": np.concatenate([high, blank], axis=1),
+        "y_back": np.concatenate([high, low, high, blank], axis=1),
         "rows": row_tables(),
         "expand": expand,
         "keep": keep,
@@ -817,7 +817,7 @@
             pltpu.VMEM((CX, C, TZ, Y), BF16),
             pltpu.VMEM((C, C), BF16),
             pltpu.VMEM((256, C), BF16),
-            pltpu.VMEM((6 * KY, 2 * Y), BF16),
+            pltpu.VMEM((80, 2 * Y), BF16),
             pltpu.VMEM((Q * TZ, 2 * K * Q), BF16),
             pltpu.VMEM((CX, C, TZ, Y), BF16),
             pltpu.VMEM((C, TZ, Y), F32),

time: 77.4 us -> 77.6 us (level)
  no operation moved by 1% of the time
where the time goes in v6:
time: 77.6 us; the launch traced here: 77.5 us
  Pallas kernels  76.7 us (99%)
  between operations  0.8 us (1%)
    pallas_call x1, Pallas kernels, per_device(): pl.pallas_call(layer_kernel, out_shape=[jax.ShapeDtypeStruct(shape, dtype...  71.7 us
    pallas_call x1, Pallas kernels, per_device(): pl.pallas_call(last_kernel, out_shape=[jax.ShapeDtypeStruct(shape, dtype)...  5.07 us

profile of v6, /device:TPU:1, one launch (start us, length us, event | category | flops | bytes accessed | tf_op | source)
XLA Modules:
  0.0 77.5 jit_solution(16236185387247396158)
XLA Ops:
  0.6 71.7 %spectral_layer.1 = (bf16[32,3,64,128]{3,2,1,0:T(8,128)(2,1)}, bf16[32,3,64,128]{3,2,1,0:T(8,128)(2,1)}, f32[2,32,8,54]{3,2,1,0:T(8,128)}, f32[3,4,24,256]{3,2,1,0:T(8,128)}, f32[32,32]{1,0:T(8,128)}) custom-call(bf16[32,3,64,128]{3,2,1,0:T(8,128)(2,1)} %bitcast.8, bf16[32,3,64,128]{3,2,1,0:T(8,128)(2,1)} %bitcast.9, bf16[512,54]{1,0:T(8,128)(2,1)} %bitcast.10, ...), custom_call_target="tpu_custom_call" | custom-call | tf_op jit(solution)/shard_map/spectral_layer/pallas_call | solution.py:798
  72.3 5.1 %last_cells.1 = (bf16[32,3,64,128]{3,2,1,0:T(8,128)(2,1)}, bf16[32,3,64,128]{3,2,1,0:T(8,128)(2,1)}, f32[2,32,8,54]{3,2,1,0:T(8,128)}, f32[32,32]{1,0:T(8,128)}) custom-call(bf16[32,3,64,128]{3,2,1,0:T(8,128)(2,1)} %get-tuple-element.13.grad_cells, f32[3,4,24,256]{3,2,1,0:T(8,128)} %get-tuple-element.14.hx, ...), custom_call_target="tpu_custom_call" | custom-call | tf_op jit(solution)/shard_map/last_cells/pallas_call | solution.py:810
